TPU v7x, 32 devices: a whole 2x2x4 slice. The times are simulated.
32 devices in a mesh: groups: 2 (over y), col: 16 (over z, x, core).
Axes of the slice: x: 2, y: 2, z: 4, core: 2. Of those that a mesh axis runs over, the one named last changes fastest.
Arguments:
- base_slab: bfloat16 [8192, 53248], P('groups', 'col'), parts along dimension 0, may hold values from -6 to 6
- down_factors: bfloat16 [4096, 4096], P(('groups', 'col')), parts along dimension 0, may hold values from -6 to 6
- up_factors: bfloat16 [4096, 53248], P(('groups', 'col')), parts along dimension 0, may hold values from -0.125 to 0.125
- mix_coeffs: float32 [64], P('groups'), parts along dimension 0, may hold values from 0.2 to 2
Outputs:
- merged_slab: bfloat16 [8192, 53248], P('groups', 'col'), parts along dimension 0
There are 2 independent parts, one for each index of `groups`. A program takes and returns all parts, laid end to end along the dimension named above; each array names one. Nothing has to cross between parts.
All inputs are finite; a program needn't handle non-finite values.
Results may differ from a plain program's by a relative error of at most 0.0038.
Values may be sent and summed in bfloat16 or wider, within the bound.
No kernel may reach another device: no remote copies, remote signals or barrier semaphores. Data moves between devices by JAX's collectives and lax.ppermute only.
A program may use at most 256 MiB of HBM per device.

v0:
```python
import jax
import jax.numpy as jnp
from jax import lax
from jax.sharding import PartitionSpec as P

RANK = 64


def contract_rank(left, right):
    return lax.dot_general(
        left, right, (((0,), (0,)), ((), ())), preferred_element_type=jnp.float32
    )


def local(base_slab, down_factors, up_factors, mix_coeffs):
    local_rank = down_factors.shape[0]
    offset = lax.axis_index("col") * local_rank
    owners = (offset + jnp.arange(local_rank, dtype=jnp.int32)) // RANK
    matches = owners[:, None] == jnp.arange(mix_coeffs.shape[0], dtype=jnp.int32)[None, :]
    per_rank = jnp.sum(jnp.where(matches, mix_coeffs[None, :], 0.0), axis=1)
    scaled = (down_factors.astype(jnp.float32) * per_rank[:, None]).astype(jnp.bfloat16)
    panels = lax.all_to_all(up_factors, "col", split_axis=1, concat_axis=0, tiled=True)
    gathered = lax.all_gather(scaled, "col", axis=0, tiled=True)
    update = contract_rank(gathered, panels)
    return (base_slab.astype(jnp.float32) + update).astype(jnp.bfloat16)


def solution(mesh):
    in_specs = (
        P("groups", "col"),
        P(("groups", "col"), None),
        P(("groups", "col"), None),
        P("groups"),
    )
    out_specs = P("groups", "col")
    return jax.shard_map(local, mesh=mesh, in_specs=in_specs, out_specs=out_specs, check_vma=False)
```

profile of v0, /device:TPU:0, one launch (start us, length us, event | category | flops | bytes accessed | tf_op | source)
XLA Modules:
  0.0 509.1 jit_solution(18230500516536464953)
XLA Ops:
  6.5 0.0 all-gather.2.cloned.1.call-start
  6.5 0.7 select_reduce_fusion
  7.3 2.5 multiply_convert_fusion
  9.8 0.0 all-gather.2.cloned.1.call-update
  9.8 18.5 %copy.7 = bf16[128,53248]{0,1:T(8,128)(2,1)} copy(bf16[128,53248]{1,0:T(8,128)(2,1)} %param.6) | data formatting | bytes 27262976 | tf_op args[2]
  28.3 389.5 %all_to_all.19 = bf16[128,16,3328]{0,2,1:T(8,128)(2,1)} all-to-all(bf16[128,16,3328]{0,2,1:T(8,128)(2,1)} %bitcast.6), channel_id=1, replica_groups=mesh['groups'=2,'col'=16] {'col'}, dimensions={1} | all-to-all | bytes 27262976 | tf_op jit(solution)/shard_map/all_to_all | solution.py:22
  417.8 17.5 %copy.8 = bf16[16,128,3328]{2,1,0:T(8,128)(2,1)} copy(bf16[16,128,3328]{1,2,0:T(8,128)(2,1)} %bitcast.5) | data formatting | bytes 27262976 | tf_op jit(solution)/shard_map/all_to_all | solution.py:22
  435.3 0.0 all-gather.2.cloned.1.call-done
  435.3 66.9 %add_convert_fusion = bf16[4096,3328]{1,0:T(8,128)(2,1)} fusion(bf16[4096,3328]{1,0:T(8,128)(2,1)} %param.4, bf16[2048,4096]{1,0:T(8,128)(2,1)} %all-gather.2.cloned.1.call-done, bf16[2048,3328]{1,0:T(8,128)(2,1)} %bitcast.7), kind=kOutput, calls=%fused_computation | convolution fusion | flops 55875469312 | bytes 84934656 | tf_op jit(solution)/shard_map/dot_general | solution.py:10
  (1 shorter events, 0.0 us)
Async XLA Ops:
  6.5 428.8 %all-gather.2.cloned.1.call-start = ((), (), s32[]{:S(2)}) async-start(), calls=%async_computation.1 | async-start | bytes 17825792 | tf_op jit(solution)/shard_map/all_gather | solution.py:23
Sparse Core Ops, SparseCore 0:
  9.9 255.2 all-gather.1
where the time goes:
time: 510 us; the launch traced here: 509 us
  blocking collectives  390 us (76%)
  matrix products  66.9 us (13%)
  local copies, waits for them, and re-layouts  36 us (7%)
  between operations  13.4 us (3%)
    all_to_all x1, blocking collectives, local(): lax.all_to_all(up_factors, 'col', split_axis=1, concat_axis=0, tiled=True)  390 us
    dot_general x1, matrix products, contract_rank(): lax.dot_general(left, right, (((0,), (0,)), ((), ())), preferred_element_...  66.9 us
    unnamed x1, local copies, waits for them, and re-layouts  18.5 us
    all_to_all x1, local copies, waits for them, and re-layouts, local(): lax.all_to_all(up_factors, 'col', split_axis=1, concat_axis=0, tiled=True)  17.5 us
  transfers between devices with their start and end apart: 1, of which 0 were waited for; matrix products, arithmetic and copies ran while one was open for 7% of the time, Pallas kernels for 0%

commit v1 on v0

v1 whole, which is shorter than its diff:
```python
import functools
import jax
import jax.numpy as jnp
from jax import lax
from jax.experimental import pallas as pl
from jax.experimental.pallas import tpu as pltpu
from jax.sharding import PartitionSpec as P

RANK = 64
UNIT = 256
ORDER = (0, 1, 2, 3, 2)
VMEM = 56 * 1024 * 1024
NO_COST = pl.CostEstimate(flops=1, bytes_accessed=1, transcendentals=0)
ANY = pl.BlockSpec(memory_space=pl.ANY)


def chunk_spans(width):
    units = width // UNIT
    if width % UNIT or units < 8:
        return [(0, width)]
    sizes = [0, 0, 0, 0]
    for i in range(units):
        sizes[ORDER[i % len(ORDER)]] += UNIT
    return [(sum(sizes[:i]), s) for i, s in enumerate(sizes)]


def assemble(plan, sources, me, depth, width, offset, w, after=()):
    up = sources["up"]
    if width % 128:
        outs = []
        for blocks in plan:
            parts = []
            for b in blocks:
                if b[0] == "own":
                    parts.append(lax.dynamic_slice(up, (0, (me ^ b[1]) * width + offset), (depth, w)))
                else:
                    parts.append(sources[b[0]][b[1]][:, b[2] : b[2] + w])
            outs.append(jnp.stack(parts))
        return outs
    tile = 32 if depth % 32 == 0 else depth
    el = pl.Element
    in_specs, operands = [], []
    for blocks in plan:
        for b in blocks:
            if b[0] == "own":
                r = b[1]
                in_specs.append(pl.BlockSpec(
                    (el(tile), el(w)),
                    lambda i, m, r=r: (i * tile, pl.multiple_of((m[0] ^ r) * width + offset, 128))))
                operands.append(up)
            else:
                lead, at = b[1], b[2]
                in_specs.append(pl.BlockSpec(
                    (el(1), el(tile), el(w)), lambda i, m, lead=lead, at=at: (lead, i * tile, at)))
                operands.append(sources[b[0]])

    def kernel(m, *refs):
        ins, outs = refs[: len(operands)], refs[len(operands) + len(after) :]
        k = 0
        for blocks, out in zip(plan, outs):
            for j in range(len(blocks)):
                out[j] = ins[k][...].reshape(tile, w)
                k += 1

    return pl.pallas_call(
        kernel,
        grid_spec=pltpu.PrefetchScalarGridSpec(
            num_scalar_prefetch=1,
            grid=(depth // tile,),
            in_specs=in_specs + [ANY] * len(after),
            out_specs=[pl.BlockSpec((len(blocks), tile, w), lambda i, m: (0, i, 0)) for blocks in plan],
        ),
        out_shape=[jax.ShapeDtypeStruct((len(blocks), depth, w), up.dtype) for blocks in plan],
        compiler_params=pltpu.CompilerParams(vmem_limit_bytes=VMEM),
        cost_estimate=NO_COST,
        name="assemble",
    )(me.reshape(1), *operands, *after)


def merge(lefts, rights, me, base, out, offset, w):
    rows, width = base.shape
    depth = rights[0].shape[1]
    tile, near, groups = 512, rights[0].shape[0], len(lefts)
    n = near * groups
    if w == width:
        slab = pl.BlockSpec((tile, w), lambda i, m: (i, 0))
    else:
        slab = pl.BlockSpec((pl.Element(tile), pl.Element(w)), lambda i, m: (i * tile, offset))

    def kernel(m, *refs):
        left, right = refs[:groups], refs[groups : 2 * groups]
        base_ref, (out_ref, panel, sem) = refs[2 * groups], refs[-3:]

        @pl.when(pl.program_id(0) == 0)
        def _():
            copies = []
            for g in range(groups):
                for j in range(near):
                    place = g * near + (m[0] ^ j) % near
                    copies.append(pltpu.make_async_copy(right[g].at[j], panel.at[place], sem.at[g * near + j]))
            for c in copies:
                c.start()
            for c in copies:
                c.wait()

        update = 0.0
        for g in range(groups):
            update += lax.dot_general(
                left[g][...],
                panel[g * near : (g + 1) * near].reshape(near * depth, w),
                (((0,), (0,)), ((), ())),
                preferred_element_type=jnp.float32,
            )
        out_ref[...] = (base_ref[...].astype(jnp.float32) + update).astype(out_ref.dtype)

    in_specs = [pl.BlockSpec((near * depth, tile), lambda i, m: (0, i))] * groups + [ANY] * groups + [slab]
    operands = [*lefts, *rights, base]
    aliases = {}
    if out is not None:
        in_specs.append(ANY)
        operands.append(out)
        aliases = {len(operands): 0}
    return pl.pallas_call(
        kernel,
        grid_spec=pltpu.PrefetchScalarGridSpec(
            num_scalar_prefetch=1,
            grid=(rows // tile,),
            in_specs=in_specs,
            out_specs=slab,
            scratch_shapes=[pltpu.VMEM((n, depth, w), base.dtype), pltpu.SemaphoreType.DMA((n,))],
        ),
        out_shape=jax.ShapeDtypeStruct(base.shape, base.dtype),
        input_output_aliases=aliases,
        compiler_params=pltpu.CompilerParams(vmem_limit_bytes=VMEM),
        cost_estimate=NO_COST,
        name="merge",
    )(me.reshape(1), *operands)


def local(n, base_slab, down_factors, up_factors, mix_coeffs):
    depth, rows = down_factors.shape
    width = base_slab.shape[1]
    quads, half = n // 4, n // 2
    me = lax.axis_index("col").astype(jnp.int32)

    def swap(v, bit):
        return lax.ppermute(v, "col", [(i, i ^ bit) for i in range(n)])

    def scale(block, source):
        owners = (source * depth + jnp.arange(depth, dtype=jnp.int32)) // RANK
        matches = owners[:, None] == jnp.arange(mix_coeffs.shape[0], dtype=jnp.int32)[None, :]
        per_rank = jnp.sum(jnp.where(matches, mix_coeffs[None, :], 0.0), axis=1)
        return (block.astype(jnp.float32) * per_rank[:, None]).astype(jnp.bfloat16)

    far = swap(down_factors, half)
    held = {0: scale(down_factors, me)}
    bit = half // 2
    while bit >= 4:
        for k in list(held):
            held[k ^ bit] = swap(held[k], bit)
        bit //= 2

    fours = [list(range(i, i + 4)) for i in range(0, n, 4)]

    def gather(v):
        return lax.all_gather(v, "col", axis_index_groups=fours, axis=0, tiled=True)

    spans = chunk_spans(width)
    last = len(spans) - 1
    w0 = spans[0][1]
    put = functools.partial(assemble, me=me, depth=depth, width=width)

    def for_core(offset, w, after):
        plan = [("own", 4 * dz + 2 * dx + 1) for dx in range(2) for dz in range(quads)]
        return put([plan], {"up": up_factors}, offset=offset, w=w, after=after)[0]

    def for_x(q, after=()):
        offset, w = spans[q]
        at = offset - w0
        plan = [b for dz in range(quads) for b in (("own", 4 * dz + 2), ("core", quads + dz, at))]
        return put([plan], {"up": up_factors, "core": got_c}, offset=offset, w=w, after=after)[0]

    def for_z(q, got_x):
        offset, w = spans[q]
        at = offset - w0
        plan = [
            [("own", 4 * dz), ("core", dz, at), ("x", 2 * dz, 0), ("x", 2 * dz + 1, 0)]
            for dz in range(quads)
        ]
        return put(plan, {"up": up_factors, "core": got_c, "x": got_x}, offset=offset, w=w)

    plan = [[("own", 4 * dz + j) for dz in range(quads)] for j in range(1, 4)]
    to_near = put(plan, {"up": up_factors}, offset=0, w=w0)
    near = [swap(v, j) for j, v in zip((1, 2, 3), to_near)]
    to_x = None
    if last:
        got_c = swap(for_core(w0, width - w0, to_near[:1]), 1)
        to_x = for_x(1)
    plan = [[("own", 4 * dz)] + [(j, dz, 0) for j in range(3)] for dz in range(quads)]
    to_z = put(plan, {"up": up_factors, **dict(enumerate(near))}, offset=0, w=w0)

    out, lefts, panels, merged = None, None, [], 0
    for q in range(last + 1):
        to_z, to_x, panels, out = lax.optimization_barrier((to_z, to_x, panels, out))
        if q == 0:
            held, far, to_z = lax.optimization_barrier((held, far, to_z))
            held[half] = scale(far, me ^ half)
            bit = half // 2
            while bit >= 4:
                for k in list(held):
                    if k >= half and k ^ bit not in held:
                        held[k ^ bit] = swap(held[k], bit)
                bit //= 2
            lefts = [gather(held[4 * dz]) for dz in range(quads)]
        if q == 2:
            lefts, panels = lax.optimization_barrier((lefts, panels))
        here = [swap(v, 4 * dz) if dz else v for dz, v in enumerate(to_z)]
        if q < last:
            got_x = swap(to_x, 2)
            to_z = for_z(q + 1, got_x)
            if q + 1 < last:
                to_x = for_x(q + 2)
        while q >= 2 and merged < q:
            out = merge(lefts, panels[merged], me, base_slab, out, *spans[merged])
            merged += 1
        panels = panels + [here]
    while merged <= last:
        out = merge(lefts, panels[merged], me, base_slab, out, *spans[merged])
        merged += 1
    return out


def solution(mesh):
    in_specs = (
        P("groups", "col"),
        P(("groups", "col"), None),
        P(("groups", "col"), None),
        P("groups"),
    )
    out_specs = P("groups", "col")
    return jax.shard_map(
        functools.partial(local, mesh.shape["col"]),
        mesh=mesh, in_specs=in_specs, out_specs=out_specs, check_vma=False,
    )
```

time: 510 us -> 461 us (0.904)
  blocking collectives: 390 us -> 0 us
  waiting for transfers between devices: 0.02 us -> 221 us
  Pallas kernels: 0 us -> 126 us
  starting transfers between devices: 0.01 us -> 85.2 us
  matrix products: 66.9 us -> 0 us
  local copies, waits for them, and re-layouts: 36 us -> 10.2 us
    all_to_all x1 -> x0, blocking collectives: 390 us -> none  [local(): lax.all_to_all(up_factors, 'col', split_axis=1, concat_axis=0, tiled=True)]
    ppermute x0 -> x22, waiting for transfers between devices: none -> 220 us  [swap(): return lax.ppermute(v, 'col', [(i, i ^ bit) for i in range(n)])]
    pallas_call x0 -> x13, Pallas kernels: none -> 126 us  [the longest x4 87.7 us: merge(): pl.pallas_call(kernel, grid_spec=pltpu.PrefetchScalarGridSpec(num_scalar_...]
    ppermute x0 -> x22, starting transfers between devices: none -> 85.1 us  [swap(): return lax.ppermute(v, 'col', [(i, i ^ bit) for i in range(n)])]
    dot_general x1 -> x0, matrix products: 66.9 us -> none  [contract_rank(): lax.dot_general(left, right, (((0,), (0,)), ((), ())), preferred_element_...]
    all_to_all x1 -> x0, local copies, waits for them, and re-layouts: 17.5 us -> none  [local(): lax.all_to_all(up_factors, 'col', split_axis=1, concat_axis=0, tiled=True)]
    unnamed x1 -> x50, local copies, waits for them, and re-layouts: 18.5 us -> 10.2 us
  transfers between devices with their start and end apart: 1 -> 26, of which waited for: 0 -> 9; matrix products, arithmetic and copies ran while one was open for 7% -> 1% of each run, Pallas kernels for 0% -> 22%
where the time goes in v1:
time: 461 us; the launch traced here: 458 us
  waiting for transfers between devices  221 us (48%)
  Pallas kernels  126 us (27%)
  starting transfers between devices  85.2 us (18%)
  between operations  13.5 us (3%)
  local copies, waits for them, and re-layouts  10.2 us (2%)
    ppermute x22, waiting for transfers between devices, swap(): return lax.ppermute(v, 'col', [(i, i ^ bit) for i in range(n)])  220 us
    pallas_call x4, Pallas kernels, merge(): pl.pallas_call(kernel, grid_spec=pltpu.PrefetchScalarGridSpec(num_scalar_...  87.7 us
    ppermute x22, starting transfers between devices, swap(): return lax.ppermute(v, 'col', [(i, i ^ bit) for i in range(n)])  85.1 us
    pallas_call x9, Pallas kernels, assemble(): pl.pallas_call(kernel, grid_spec=pltpu.PrefetchScalarGridSpec(num_scalar_...  37.9 us
    unnamed x50, local copies, waits for them, and re-layouts  10.2 us
  transfers between devices with their start and end apart: 26, of which 9 were waited for; matrix products, arithmetic and copies ran while one was open for 1% of the time, Pallas kernels for 22%

profile of v1, /device:TPU:0, one launch (start us, length us, event | category | flops | bytes accessed | tf_op | source)
XLA Modules:
  0.0 458.0 jit_solution(10434829233612557193)
XLA Ops:
  6.5 4.0 assemble.9
  10.5 5.5 %assemble.11 = bf16[8,128,2560]{2,1,0:T(8,128)(2,1)} custom-call(s32[1]{0:T(128)} %bitcast.m, bf16[128,53248]{1,0:T(8,128)(2,1)} %refs_12_.7, bf16[128,53248]{1,0:T(8,128)(2,1)} %refs_12_.7, bf16[128,53248]{1,0:T(8,128)(2,1)} %refs_12_.7, bf16[128,53248]{1,0:T(8,128)(2,1)} %refs_12_.7, bf16[128,53248]{1,0:T(8,128)(2,1)} %refs_12_.7, ...), custom_call_target="tpu_custom_call" | custom-call | flops 1 | bytes 1 | tf_op jit(solution)/shard_map/assemble/pallas_call | solution.py:65
  23.7 14.0 %collective-permute-done.3.refs_2_.refs_6_.refs_10_.refs_14_ = bf16[4,128,768]{2,1,0:T(8,128)(2,1)S(1)} collective-permute-done((bf16[4,128,768]{2,1,0:T(8,128)(2,1)}, bf16[4,128,768]{2,1,0:T(8,128)(2,1)S(1)}, u32[]{:S(2)}, u32[]{:S(2)}) %collective-permute-start.3) | collective-permute-done | bytes 786464 | tf_op jit(solution)/shard_map/ppermute | solution.py:147
  37.6 16.3 %collective-permute-done.4.refs_3_.refs_7_.refs_11_.refs_15_ = bf16[4,128,768]{2,1,0:T(8,128)(2,1)S(1)} collective-permute-done((bf16[4,128,768]{2,1,0:T(8,128)(2,1)}, bf16[4,128,768]{2,1,0:T(8,128)(2,1)S(1)}, u32[]{:S(2)}, u32[]{:S(2)}) %collective-permute-start.4) | collective-permute-done | bytes 786464 | tf_op jit(solution)/shard_map/ppermute | solution.py:147
  55.7 4.2 assemble.10
  59.9 3.6 assemble.12
  63.5 3.7 collective-permute-done
  73.5 22.8 %collective-permute-done.6 = bf16[128,4096]{1,0:T(8,128)(2,1)S(1)} collective-permute-done((bf16[128,4096]{1,0:T(8,128)(2,1)}, bf16[128,4096]{1,0:T(8,128)(2,1)S(1)}, u32[]{:S(2)}, u32[]{:S(2)}) %collective-permute-start.6) | collective-permute-done | bytes 1048608 | tf_op jit(solution)/shard_map/ppermute | solution.py:147
  102.3 4.1 assemble.14
  106.4 47.5 %collective-permute-done.7.refs_2_.refs_3_.refs_6_.refs_7_.refs_10_.refs_11_.refs_14_.refs_15_ = bf16[8,128,768]{2,1,0:T(8,128)(2,1)S(1)} collective-permute-done((bf16[8,128,768]{2,1,0:T(8,128)(2,1)S(1)}, bf16[8,128,768]{2,1,0:T(8,128)(2,1)S(1)}, u32[]{:S(2)}, u32[]{:S(2)}) %collective-permute-start.7) | collective-permute-done | bytes 1572896 | tf_op jit(solution)/shard_map/ppermute | solution.py:147
  155.1 4.2 assemble.13
  160.6 10.4 %collective-permute-start.12 = (bf16[4,128,768]{2,1,0:T(8,128)(2,1)}, bf16[4,128,768]{2,1,0:T(8,128)(2,1)S(1)}, u32[]{:S(2)}, u32[]{:S(2)}) collective-permute-start(bf16[4,128,768]{2,1,0:T(8,128)(2,1)} %get-tuple-element.112), channel_id=1, source_target_pairs={{0,4},{1,5},{2,6},{3,7},{4,0},{5,1},{6,2},{7,3},{8,12},{9,13},{10,... | collective-permute-start | bytes 2359304 | tf_op jit(solution)/shard_map/ppermute | solution.py:147
  173.3 3.2 assemble.16
  176.5 74.2 %collective-permute-done.11.refs_2_.refs_3_.refs_6_.refs_7_.refs_10_.refs_11_.refs_14_.refs_15_ = bf16[8,128,1280]{2,1,0:T(8,128)(2,1)S(1)} collective-permute-done((bf16[8,128,1280]{2,1,0:T(8,128)(2,1)S(1)}, bf16[8,128,1280]{2,1,0:T(8,128)(2,1)S(1)}, u32[]{:S(2)}, u32[]{:S(2)}) %collective-permute-start.11) | collective-permute-done | bytes 2621472 | tf_op jit(solution)/shard_map/ppermute | solution.py:147
  252.3 5.5 %assemble.15 = (bf16[4,128,1280]{2,1,0:T(8,128)(2,1)}, bf16[4,128,1280]{2,1,0:T(8,128)(2,1)}, bf16[4,128,1280]{2,1,0:T(8,128)(2,1)}, bf16[4,128,1280]{2,1,0:T(8,128)(2,1)}) custom-call(s32[1]{0:T(128)} %bitcast.m, bf16[128,53248]{1,0:T(8,128)(2,1)} %refs_12_.7, bf16[8,128,2560]{2,1,0:T(8,128)(2,1)} %collective-permute-done.5.refs_1_.refs_3_.refs_5_.refs_7_.refs_9_.refs_13_, ...), custom_call_target="tpu_custom_call" | custom-call | flops 1 | bytes 1 | tf_op jit(solution)/shard_map/assemble/pallas_call | solution.py:65
  259.0 16.9 %collective-permute-start.16 = (bf16[4,128,1280]{2,1,0:T(8,128)(2,1)}, bf16[4,128,1280]{2,1,0:T(8,128)(2,1)S(1)}, u32[]{:S(2)}, u32[]{:S(2)}) collective-permute-start(bf16[4,128,1280]{2,1,0:T(8,128)(2,1)} %get-tuple-element.141), channel_id=1, source_target_pairs={{0,4},{1,5},{2,6},{3,7},{4,0},{5,1},{6,2},{7,3},{8,12},{9,13},{10,... | collective-permute-start | bytes 3932168 | tf_op jit(solution)/shard_map/ppermute | solution.py:147
  279.9 13.3 %collective-permute-done.15.refs_2_.refs_3_.refs_6_.refs_7_.refs_10_.refs_11_.refs_14_.refs_15_ = bf16[8,128,512]{2,1,0:T(8,128)(2,1)S(1)} collective-permute-done((bf16[8,128,512]{2,1,0:T(8,128)(2,1)S(1)}, bf16[8,128,512]{2,1,0:T(8,128)(2,1)S(1)}, u32[]{:S(2)}, u32[]{:S(2)}) %collective-permute-start.15) | collective-permute-done | bytes 1048608 | tf_op jit(solution)/shard_map/ppermute | solution.py:147
  294.2 3.7 assemble.17
  298.0 20.5 %merge.4.refs_9_ = bf16[4096,3328]{1,0:T(8,128)(2,1)} custom-call(s32[1]{0:T(128)} %bitcast.m, bf16[512,4096]{1,0:T(8,128)(2,1)} %all-gather.5.cloned.1.call-done.refs_0_, bf16[512,4096]{1,0:T(8,128)(2,1)} %all-gather.7.cloned.1.call-done.refs_1_, bf16[512,4096]{1,0:T(8,128)(2,1)} %all-gather.9.cloned.1.call-done.refs_2_, ...), custom_call_target="tpu_custom_call" | custom-call | flops 1 | bytes 1 | tf_op jit(solution)/shard_map/merge/pallas_call | solution.py:123
  318.5 20.9 %merge.5.refs_9_ = bf16[4096,3328]{1,0:T(8,128)(2,1)} custom-call(s32[1]{0:T(128)} %bitcast.m, bf16[512,4096]{1,0:T(8,128)(2,1)} %all-gather.5.cloned.1.call-done.refs_0_, bf16[512,4096]{1,0:T(8,128)(2,1)} %all-gather.7.cloned.1.call-done.refs_1_, bf16[512,4096]{1,0:T(8,128)(2,1)} %all-gather.9.cloned.1.call-done.refs_2_, ...), custom_call_target="tpu_custom_call", output_to_operand_aliasing={{}: (10, {})} | custom-call | flops 1 | bytes 1 | tf_op jit(solution)/shard_map/merge/pallas_call | solution.py:123
  339.4 25.4 %collective-permute-done.17.refs_6_ = bf16[4,128,1280]{2,1,0:T(8,128)(2,1)S(1)} collective-permute-done((bf16[4,128,1280]{2,1,0:T(8,128)(2,1)}, bf16[4,128,1280]{2,1,0:T(8,128)(2,1)S(1)}, u32[]{:S(2)}, u32[]{:S(2)}) %collective-permute-start.17) | collective-permute-done | bytes 1310752 | tf_op jit(solution)/shard_map/ppermute | solution.py:147
  364.9 35.9 %collective-permute-start.19 = (bf16[4,128,512]{2,1,0:T(8,128)(2,1)S(1)}, bf16[4,128,512]{2,1,0:T(8,128)(2,1)S(1)}, u32[]{:S(2)}, u32[]{:S(2)}) collective-permute-start(bf16[4,128,512]{2,1,0:T(8,128)(2,1)S(1)} %copy-done.24), channel_id=1, source_target_pairs={{0,4},{1,5},{2,6},{3,7},{4,0},{5,1},{6,2},{7,3},{8,12},{9,13},{10,... | collective-permute-start | bytes 1572872 | tf_op jit(solution)/shard_map/ppermute | solution.py:147
  403.2 29.6 %merge.6.refs_9_ = bf16[4096,3328]{1,0:T(8,128)(2,1)} custom-call(s32[1]{0:T(128)} %bitcast.m, bf16[512,4096]{1,0:T(8,128)(2,1)} %all-gather.5.cloned.1.call-done.refs_0_, bf16[512,4096]{1,0:T(8,128)(2,1)} %all-gather.7.cloned.1.call-done.refs_1_, bf16[512,4096]{1,0:T(8,128)(2,1)} %all-gather.9.cloned.1.call-done.refs_2_, ...), custom_call_target="tpu_custom_call", output_to_operand_aliasing={{}: (10, {})} | custom-call | flops 1 | bytes 1 | tf_op jit(solution)/shard_map/merge/pallas_call | solution.py:123
  434.7 16.7 %merge.7 = bf16[4096,3328]{1,0:T(8,128)(2,1)} custom-call(s32[1]{0:T(128)} %bitcast.m, bf16[512,4096]{1,0:T(8,128)(2,1)} %all-gather.5.cloned.1.call-done.refs_0_, bf16[512,4096]{1,0:T(8,128)(2,1)} %all-gather.7.cloned.1.call-done.refs_1_, bf16[512,4096]{1,0:T(8,128)(2,1)} %all-gather.9.cloned.1.call-done.refs_2_, ...), custom_call_target="tpu_custom_call", output_to_operand_aliasing={{}: (10, {})} | custom-call | flops 1 | bytes 1 | tf_op jit(solution)/shard_map/merge/pallas_call | solution.py:123
  (100 shorter events, 38.4 us)
Async XLA Ops:
  6.5 291.4 %all-gather.5.cloned.1.call-start = ((), (), s32[]{:S(2)}) async-start(), calls=%async_computation | async-start | bytes 5242880 | tf_op jit(solution)/shard_map/all_gather | solution.py:166
  16.0 43.9 %collective-permute-start.5 = (bf16[8,128,2560]{2,1,0:T(8,128)(2,1)}, bf16[8,128,2560]{2,1,0:T(8,128)(2,1)}, u32[]{:S(2)}, u32[]{:S(2)}) collective-permute-start(bf16[8,128,2560]{2,1,0:T(8,128)(2,1)} %assemble.11), channel_id=1, source_target_pairs={{0,1},{1,0},{2,3},{3,2},{4,5},{5,4},{6,7},{7,6},{8,9},{9,8},{10,11... | collective-permute-start | bytes 15728648 | tf_op jit(solution)/shard_map/ppermute | solution.py:147
  16.5 21.2 %collective-permute-start.3 = (bf16[4,128,768]{2,1,0:T(8,128)(2,1)}, bf16[4,128,768]{2,1,0:T(8,128)(2,1)S(1)}, u32[]{:S(2)}, u32[]{:S(2)}) collective-permute-start(bf16[4,128,768]{2,1,0:T(8,128)(2,1)} %get-tuple-element.80), channel_id=1, source_target_pairs={{0,2},{1,3},{2,0},{3,1},{4,6},{5,7},{6,4},{7,5},{8,10},{9,11},{10,... | collective-permute-start | bytes 2359304 | tf_op jit(solution)/shard_map/ppermute | solution.py:147
  19.4 47.8 %collective-permute-start = (bf16[128,4096]{1,0:T(8,128)(2,1)S(1)}, bf16[128,4096]{1,0:T(8,128)(2,1)}, u32[]{:S(2)}, u32[]{:S(2)}) collective-permute-start(bf16[128,4096]{1,0:T(8,128)(2,1)S(1)} %multiply_convert_fusion.1), channel_id=1, source_target_pairs={{0,4},{1,5},{2,6},{3,7},{4,0},{5,1},{6,2},{7,3},{8,12},{9,13},{10,... | collective-permute-start | bytes 3145736 | tf_op jit(solution)/shard_map/ppermute | solution.py:147
  21.1 48.5 %collective-permute-start.1 = (bf16[128,4096]{1,0:T(8,128)(2,1)S(1)}, bf16[128,4096]{1,0:T(8,128)(2,1)}, u32[]{:S(2)}, u32[]{:S(2)}) collective-permute-start(bf16[128,4096]{1,0:T(8,128)(2,1)S(1)} %copy-done.12), channel_id=1, source_target_pairs={{0,8},{1,9},{2,10},{3,11},{4,12},{5,13},{6,14},{7,15},{8,0},{9,1},... | collective-permute-start | bytes 3145736 | tf_op jit(solution)/shard_map/ppermute | solution.py:147
  23.7 30.3 %collective-permute-start.4 = (bf16[4,128,768]{2,1,0:T(8,128)(2,1)}, bf16[4,128,768]{2,1,0:T(8,128)(2,1)S(1)}, u32[]{:S(2)}, u32[]{:S(2)}) collective-permute-start(bf16[4,128,768]{2,1,0:T(8,128)(2,1)} %get-tuple-element.81), channel_id=1, source_target_pairs={{0,3},{1,2},{2,1},{3,0},{4,7},{5,6},{6,5},{7,4},{8,11},{9,10},{10,... | collective-permute-start | bytes 2359304 | tf_op jit(solution)/shard_map/ppermute | solution.py:147
  69.6 228.4 %all-gather.7.cloned.1.call-start = ((), (), s32[]{:S(2)}) async-start(), calls=%async_computation.1 | async-start | bytes 5242880 | tf_op jit(solution)/shard_map/all_gather | solution.py:166
  70.3 227.7 %all-gather.9.cloned.1.call-start = ((), (), s32[]{:S(2)}) async-start(), calls=%async_computation.2 | async-start | bytes 5242880 | tf_op jit(solution)/shard_map/all_gather | solution.py:166
  73.0 225.1 %all-gather.11.cloned.1.call-start = ((), (), s32[]{:S(2)}) async-start(), calls=%async_computation.3 | async-start | bytes 5242880 | tf_op jit(solution)/shard_map/all_gather | solution.py:166
  73.0 23.3 %collective-permute-start.6 = (bf16[128,4096]{1,0:T(8,128)(2,1)}, bf16[128,4096]{1,0:T(8,128)(2,1)S(1)}, u32[]{:S(2)}, u32[]{:S(2)}) collective-permute-start(bf16[128,4096]{1,0:T(8,128)(2,1)} %multiply_convert_fusion), channel_id=1, source_target_pairs={{0,4},{1,5},{2,6},{3,7},{4,0},{5,1},{6,2},{7,3},{8,12},{9,13},{10,... | collective-permute-start | bytes 3145736 | tf_op jit(solution)/shard_map/ppermute | solution.py:147
  97.4 56.6 %collective-permute-start.7 = (bf16[8,128,768]{2,1,0:T(8,128)(2,1)S(1)}, bf16[8,128,768]{2,1,0:T(8,128)(2,1)S(1)}, u32[]{:S(2)}, u32[]{:S(2)}) collective-permute-start(bf16[8,128,768]{2,1,0:T(8,128)(2,1)S(1)} %copy-done.8), channel_id=1, source_target_pairs={{0,2},{1,3},{2,0},{3,1},{4,6},{5,7},{6,4},{7,5},{8,10},{9,11},{10,... | collective-permute-start | bytes 4718600 | tf_op jit(solution)/shard_map/ppermute | solution.py:147
  98.0 61.3 %collective-permute-start.8 = (bf16[4,128,768]{2,1,0:T(8,128)(2,1)}, bf16[4,128,768]{2,1,0:T(8,128)(2,1)S(1)}, u32[]{:S(2)}, u32[]{:S(2)}) collective-permute-start(bf16[4,128,768]{2,1,0:T(8,128)(2,1)} %get-tuple-element.99), channel_id=1, source_target_pairs={{0,4},{1,5},{2,6},{3,7},{4,0},{5,1},{6,2},{7,3},{8,12},{9,13},{10,... | collective-permute-start | bytes 2359304 | tf_op jit(solution)/shard_map/ppermute | solution.py:147
  99.7 59.6 %collective-permute-start.9 = (bf16[4,128,768]{2,1,0:T(8,128)(2,1)}, bf16[4,128,768]{2,1,0:T(8,128)(2,1)S(1)}, u32[]{:S(2)}, u32[]{:S(2)}) collective-permute-start(bf16[4,128,768]{2,1,0:T(8,128)(2,1)} %get-tuple-element.100), channel_id=1, source_target_pairs={{0,8},{1,9},{2,10},{3,11},{4,12},{5,13},{6,14},{7,15},{8,0},{9,1},... | collective-permute-start | bytes 2359304 | tf_op jit(solution)/shard_map/ppermute | solution.py:147
  102.1 57.3 %collective-permute-start.10 = (bf16[4,128,768]{2,1,0:T(8,128)(2,1)}, bf16[4,128,768]{2,1,0:T(8,128)(2,1)}, u32[]{:S(2)}, u32[]{:S(2)}) collective-permute-start(bf16[4,128,768]{2,1,0:T(8,128)(2,1)} %get-tuple-element.101), channel_id=1, source_target_pairs={{0,12},{1,13},{2,14},{3,15},{4,8},{5,9},{6,10},{7,11},{8,4},{9,5},... | collective-permute-start | bytes 2359304 | tf_op jit(solution)/shard_map/ppermute | solution.py:147
  160.2 90.5 %collective-permute-start.11 = (bf16[8,128,1280]{2,1,0:T(8,128)(2,1)S(1)}, bf16[8,128,1280]{2,1,0:T(8,128)(2,1)S(1)}, u32[]{:S(2)}, u32[]{:S(2)}) collective-permute-start(bf16[8,128,1280]{2,1,0:T(8,128)(2,1)S(1)} %copy-done.7), channel_id=1, source_target_pairs={{0,2},{1,3},{2,0},{3,1},{4,6},{5,7},{6,4},{7,5},{8,10},{9,11},{10,... | collective-permute-start | bytes 7864328 | tf_op jit(solution)/shard_map/ppermute | solution.py:147
  160.6 97.2 %collective-permute-start.12 = (bf16[4,128,768]{2,1,0:T(8,128)(2,1)}, bf16[4,128,768]{2,1,0:T(8,128)(2,1)S(1)}, u32[]{:S(2)}, u32[]{:S(2)}) collective-permute-start(bf16[4,128,768]{2,1,0:T(8,128)(2,1)} %get-tuple-element.112), channel_id=1, source_target_pairs={{0,4},{1,5},{2,6},{3,7},{4,0},{5,1},{6,2},{7,3},{8,12},{9,13},{10,... | collective-permute-start | bytes 2359304 | tf_op jit(solution)/shard_map/ppermute | solution.py:147
  170.9 86.9 %collective-permute-start.13 = (bf16[4,128,768]{2,1,0:T(8,128)(2,1)}, bf16[4,128,768]{2,1,0:T(8,128)(2,1)S(1)}, u32[]{:S(2)}, u32[]{:S(2)}) collective-permute-start(bf16[4,128,768]{2,1,0:T(8,128)(2,1)} %get-tuple-element.113), channel_id=1, source_target_pairs={{0,8},{1,9},{2,10},{3,11},{4,12},{5,13},{6,14},{7,15},{8,0},{9,1},... | collective-permute-start | bytes 2359304 | tf_op jit(solution)/shard_map/ppermute | solution.py:147
  171.6 86.2 %collective-permute-start.14 = (bf16[4,128,768]{2,1,0:T(8,128)(2,1)}, bf16[4,128,768]{2,1,0:T(8,128)(2,1)}, u32[]{:S(2)}, u32[]{:S(2)}) collective-permute-start(bf16[4,128,768]{2,1,0:T(8,128)(2,1)} %get-tuple-element.114), channel_id=1, source_target_pairs={{0,12},{1,13},{2,14},{3,15},{4,8},{5,9},{6,10},{7,11},{8,4},{9,5},... | collective-permute-start | bytes 2359304 | tf_op jit(solution)/shard_map/ppermute | solution.py:147
  259.0 80.5 %collective-permute-start.16 = (bf16[4,128,1280]{2,1,0:T(8,128)(2,1)}, bf16[4,128,1280]{2,1,0:T(8,128)(2,1)S(1)}, u32[]{:S(2)}, u32[]{:S(2)}) collective-permute-start(bf16[4,128,1280]{2,1,0:T(8,128)(2,1)} %get-tuple-element.141), channel_id=1, source_target_pairs={{0,4},{1,5},{2,6},{3,7},{4,0},{5,1},{6,2},{7,3},{8,12},{9,13},{10,... | collective-permute-start | bytes 3932168 | tf_op jit(solution)/shard_map/ppermute | solution.py:147
  275.9 89.0 %collective-permute-start.17 = (bf16[4,128,1280]{2,1,0:T(8,128)(2,1)}, bf16[4,128,1280]{2,1,0:T(8,128)(2,1)S(1)}, u32[]{:S(2)}, u32[]{:S(2)}) collective-permute-start(bf16[4,128,1280]{2,1,0:T(8,128)(2,1)} %get-tuple-element.142), channel_id=1, source_target_pairs={{0,8},{1,9},{2,10},{3,11},{4,12},{5,13},{6,14},{7,15},{8,0},{9,1},... | collective-permute-start | bytes 3932168 | tf_op jit(solution)/shard_map/ppermute | solution.py:147
  276.4 88.5 %collective-permute-start.18 = (bf16[4,128,1280]{2,1,0:T(8,128)(2,1)}, bf16[4,128,1280]{2,1,0:T(8,128)(2,1)}, u32[]{:S(2)}, u32[]{:S(2)}) collective-permute-start(bf16[4,128,1280]{2,1,0:T(8,128)(2,1)} %get-tuple-element.143), channel_id=1, source_target_pairs={{0,12},{1,13},{2,14},{3,15},{4,8},{5,9},{6,10},{7,11},{8,4},{9,5},... | collective-permute-start | bytes 3932168 | tf_op jit(solution)/shard_map/ppermute | solution.py:147
  364.9 68.0 %collective-permute-start.19 = (bf16[4,128,512]{2,1,0:T(8,128)(2,1)S(1)}, bf16[4,128,512]{2,1,0:T(8,128)(2,1)S(1)}, u32[]{:S(2)}, u32[]{:S(2)}) collective-permute-start(bf16[4,128,512]{2,1,0:T(8,128)(2,1)S(1)} %copy-done.24), channel_id=1, source_target_pairs={{0,4},{1,5},{2,6},{3,7},{4,0},{5,1},{6,2},{7,3},{8,12},{9,13},{10,... | collective-permute-start | bytes 1572872 | tf_op jit(solution)/shard_map/ppermute | solution.py:147
  400.8 32.1 %collective-permute-start.20 = (bf16[4,128,512]{2,1,0:T(8,128)(2,1)S(1)}, bf16[4,128,512]{2,1,0:T(8,128)(2,1)S(1)}, u32[]{:S(2)}, u32[]{:S(2)}) collective-permute-start(bf16[4,128,512]{2,1,0:T(8,128)(2,1)S(1)} %copy-done.23), channel_id=1, source_target_pairs={{0,8},{1,9},{2,10},{3,11},{4,12},{5,13},{6,14},{7,15},{8,0},{9,1},... | collective-permute-start | bytes 1572872 | tf_op jit(solution)/shard_map/ppermute | solution.py:147
  401.4 31.5 %collective-permute-start.21 = (bf16[4,128,512]{2,1,0:T(8,128)(2,1)S(1)}, bf16[4,128,512]{2,1,0:T(8,128)(2,1)S(1)}, u32[]{:S(2)}, u32[]{:S(2)}) collective-permute-start(bf16[4,128,512]{2,1,0:T(8,128)(2,1)S(1)} %copy-done.22), channel_id=1, source_target_pairs={{0,12},{1,13},{2,14},{3,15},{4,8},{5,9},{6,10},{7,11},{8,4},{9,5},... | collective-permute-start | bytes 1572872 | tf_op jit(solution)/shard_map/ppermute | solution.py:147
  (27 other events, 555.0 us)
Sparse Core Ops, SparseCore 0:
  69.7 36.8 all-gather.4
  108.1 51.3 all-gather.6
  161.1 57.0 all-gather.8
  219.6 42.8 all-gather.10

commit v2 on v1

v2 whole, which is shorter than its diff:
```python
import functools
import jax
import jax.numpy as jnp
from jax import lax
from jax.experimental import pallas as pl
from jax.experimental.pallas import tpu as pltpu
from jax.sharding import PartitionSpec as P

RANK = 64
UNIT = 256
ORDER = (0, 1, 2, 3, 0, 1, 2, 3, 0, 1, 2, 0, 1)
VMEM = 56 * 1024 * 1024
NO_COST = pl.CostEstimate(flops=1, bytes_accessed=1, transcendentals=0)
ANY = pl.BlockSpec(memory_space=pl.ANY)


def chunk_spans(width):
    units = width // UNIT
    if width % UNIT or units < 8:
        return [(0, width)]
    sizes = [0, 0, 0, 0]
    for i in range(units):
        sizes[ORDER[i % len(ORDER)]] += UNIT
    return [(sum(sizes[:i]), s) for i, s in enumerate(sizes)]


def assemble(plan, sources, me, depth, width):
    up = sources["up"]
    if width % 128:
        outs = []
        for offset, w, blocks in plan:
            parts = []
            for b in blocks:
                if b[0] == "own":
                    parts.append(lax.dynamic_slice(up, (0, (me ^ b[1]) * width + offset), (depth, w)))
                else:
                    parts.append(sources[b[0]][b[1]][:, b[2] : b[2] + w])
            outs.append(jnp.stack(parts))
        return outs
    tile = 32 if depth % 32 == 0 else depth
    el = pl.Element
    in_specs, operands = [], []
    for offset, w, blocks in plan:
        for b in blocks:
            if b[0] == "own":
                in_specs.append(pl.BlockSpec(
                    (el(tile), el(w)),
                    lambda i, m, r=b[1], offset=offset: (
                        i * tile, pl.multiple_of((m[0] ^ r) * width + offset, 128))))
                operands.append(up)
            else:
                in_specs.append(pl.BlockSpec(
                    (el(1), el(tile), el(w)), lambda i, m, lead=b[1], at=b[2]: (lead, i * tile, at)))
                operands.append(sources[b[0]])

    def kernel(m, *refs):
        ins, outs = refs[: len(operands)], refs[len(operands) :]
        k = 0
        for (_, w, blocks), out in zip(plan, outs):
            for j in range(len(blocks)):
                out[j] = ins[k][...].reshape(tile, w)
                k += 1

    return pl.pallas_call(
        kernel,
        grid_spec=pltpu.PrefetchScalarGridSpec(
            num_scalar_prefetch=1,
            grid=(depth // tile,),
            in_specs=in_specs,
            out_specs=[pl.BlockSpec((len(blocks), tile, w), lambda i, m: (0, i, 0)) for _, w, blocks in plan],
        ),
        out_shape=[jax.ShapeDtypeStruct((len(blocks), depth, w), up.dtype) for _, w, blocks in plan],
        compiler_params=pltpu.CompilerParams(vmem_limit_bytes=VMEM),
        cost_estimate=NO_COST,
        name="assemble",
    )(me.reshape(1), *operands)


def merge(lefts, rights, me, base, out, offset, w):
    rows, width = base.shape
    depth = rights[0].shape[1]
    tile, near, groups = 512, rights[0].shape[0], len(lefts)
    n = near * groups
    if w == width:
        slab = pl.BlockSpec((tile, w), lambda i, m: (i, 0))
    else:
        slab = pl.BlockSpec((pl.Element(tile), pl.Element(w)), lambda i, m: (i * tile, offset))

    def kernel(m, *refs):
        left, right = refs[:groups], refs[groups : 2 * groups]
        base_ref, (out_ref, panel, sem) = refs[2 * groups], refs[-3:]

        @pl.when(pl.program_id(0) == 0)
        def _():
            copies = []
            for g in range(groups):
                for j in range(near):
                    place = g * near + (m[0] ^ j) % near
                    copies.append(pltpu.make_async_copy(right[g].at[j], panel.at[place], sem.at[g * near + j]))
            for c in copies:
                c.start()
            for c in copies:
                c.wait()

        update = 0.0
        for g in range(groups):
            update += lax.dot_general(
                left[g][...],
                panel[g * near : (g + 1) * near].reshape(near * depth, w),
                (((0,), (0,)), ((), ())),
                preferred_element_type=jnp.float32,
            )
        out_ref[...] = (base_ref[...].astype(jnp.float32) + update).astype(out_ref.dtype)

    in_specs = [pl.BlockSpec((near * depth, tile), lambda i, m: (0, i))] * groups + [ANY] * groups + [slab]
    operands = [*lefts, *rights, base]
    aliases = {}
    if out is not None:
        in_specs.append(ANY)
        operands.append(out)
        aliases = {len(operands): 0}
    return pl.pallas_call(
        kernel,
        grid_spec=pltpu.PrefetchScalarGridSpec(
            num_scalar_prefetch=1,
            grid=(rows // tile,),
            in_specs=in_specs,
            out_specs=slab,
            scratch_shapes=[pltpu.VMEM((n, depth, w), base.dtype), pltpu.SemaphoreType.DMA((n,))],
        ),
        out_shape=jax.ShapeDtypeStruct(base.shape, base.dtype),
        input_output_aliases=aliases,
        compiler_params=pltpu.CompilerParams(vmem_limit_bytes=VMEM),
        cost_estimate=NO_COST,
        name="merge",
    )(me.reshape(1), *operands)


def local(n, base_slab, down_factors, up_factors, mix_coeffs):
    depth, rows = down_factors.shape
    width = base_slab.shape[1]
    quads, half = n // 4, n // 2
    me = lax.axis_index("col").astype(jnp.int32)

    def swap(v, bit):
        return lax.ppermute(v, "col", [(i, i ^ bit) for i in range(n)])

    owners = (me * depth + jnp.arange(depth, dtype=jnp.int32)) // RANK
    matches = owners[:, None] == jnp.arange(mix_coeffs.shape[0], dtype=jnp.int32)[None, :]
    per_rank = jnp.sum(jnp.where(matches, mix_coeffs[None, :], 0.0), axis=1)
    scaled = (down_factors.astype(jnp.float32) * per_rank[:, None]).astype(jnp.bfloat16)

    def across(v, at):
        got, bit = {at: v}, half // 2
        while bit >= 4:
            got.update({k ^ bit: swap(b, bit) for k, b in list(got.items())})
            bit //= 2
        return got

    far = swap(scaled, half)
    held = across(scaled, 0)
    fours = [list(range(i, i + 4)) for i in range(0, n, 4)]

    def gather(v):
        return lax.all_gather(v, "col", axis_index_groups=fours, axis=0, tiled=True)

    spans = chunk_spans(width)
    last = len(spans) - 1
    w0 = spans[0][1]
    put = functools.partial(assemble, me=me, depth=depth, width=width)

    to_core = [("own", 4 * dz + 2 * dx + 1) for dx in range(2) for dz in range(quads)]
    to_2, to_3, to_1 = put(
        [(0, w0, [("own", 4 * dz + j) for dz in range(quads)]) for j in (2, 3)] + [(0, width, to_core)],
        {"up": up_factors},
    )
    got_2, got_3, got_c = swap(to_2, 2), swap(to_3, 3), swap(to_1, 1)
    src = {"up": up_factors, "core": got_c, 2: got_2, 3: got_3}

    def for_x(q):
        offset, w = spans[q]
        plan = [b for dz in range(quads) for b in (("own", 4 * dz + 2), ("core", quads + dz, offset))]
        return put([(offset, w, plan)], src)[0]

    def for_z(q, got_x):
        offset, w = spans[q]
        return put([
            (offset, w, [("own", 4 * dz), ("core", dz, offset), ("x", 2 * dz, 0), ("x", 2 * dz + 1, 0)])
            for dz in range(quads)
        ], {**src, "x": got_x})

    to_x = for_x(1) if last else None
    to_z = put([
        (0, w0, [("own", 4 * dz), ("core", dz, 0), (2, dz, 0), (3, dz, 0)]) for dz in range(quads)
    ], src)

    out, panels, merged = None, [], 0
    far, held, to_z, to_x = lax.optimization_barrier((far, held, to_z, to_x))
    lefts = {k: gather(v) for k, v in held.items()}
    lefts[half] = gather(far)
    far_held = across(far, half)
    for q in range(last + 1):
        if q:
            to_z, to_x, panels, out = lax.optimization_barrier((to_z, to_x, panels, out))
        if q == min(1, last):
            far_held, to_z, panels = lax.optimization_barrier((far_held, to_z, panels))
            lefts.update({k: gather(v) for k, v in far_held.items() if k != half})
        here = [swap(v, 4 * dz) if dz else v for dz, v in enumerate(to_z)]
        if q < last:
            got_x = swap(to_x, 2)
            to_z = for_z(q + 1, got_x)
            if q + 1 < last:
                to_x = for_x(q + 2)
        if q == min(2, last):
            lefts, panels = lax.optimization_barrier((lefts, panels))
            left = [lefts[4 * dz] for dz in range(quads)]
        panels = panels + [here]
        while merged < (q if q >= 2 and q < last else q + 1 if q == last else 0):
            out = merge(left, panels[merged], me, base_slab, out, *spans[merged])
            merged += 1
    return out


def solution(mesh):
    in_specs = (
        P("groups", "col"),
        P(("groups", "col"), None),
        P(("groups", "col"), None),
        P("groups"),
    )
    out_specs = P("groups", "col")
    return jax.shard_map(
        functools.partial(local, mesh.shape["col"]),
        mesh=mesh, in_specs=in_specs, out_specs=out_specs, check_vma=False,
    )
```

time: 461 us -> 409 us (0.89)
  starting transfers between devices: 85.2 us -> 50.6 us
  waiting for transfers between devices: 221 us -> 208 us
    ppermute x22 -> x21, starting transfers between devices: 85.1 us -> 50.5 us  [swap(): return lax.ppermute(v, 'col', [(i, i ^ bit) for i in range(n)])]
    ppermute x22 -> x21, waiting for transfers between devices: 220 us -> 207 us  [swap(): return lax.ppermute(v, 'col', [(i, i ^ bit) for i in range(n)])]
    unnamed x50 -> x44, local copies, waits for them, and re-layouts: 10.2 us -> 6.2 us
    pallas_call x9 -> x8, Pallas kernels: 37.9 us -> 35.6 us  [assemble(): pl.pallas_call(kernel, grid_spec=pltpu.PrefetchScalarGridSpec(num_scalar_...]
  transfers between devices with their start and end apart: 26 -> 25, of which waited for: 9 -> 10; matrix products, arithmetic and copies ran while one was open for 1% -> 0% of each run, Pallas kernels for 22% -> 24%
where the time goes in v2:
time: 409 us; the launch traced here: 403 us
  waiting for transfers between devices  208 us (51%)
  Pallas kernels  122 us (30%)
  starting transfers between devices  50.6 us (12%)
  between operations  13.5 us (3%)
  local copies, waits for them, and re-layouts  6.2 us (2%)
    ppermute x21, waiting for transfers between devices, swap(): return lax.ppermute(v, 'col', [(i, i ^ bit) for i in range(n)])  207 us
    pallas_call x4, Pallas kernels, merge(): pl.pallas_call(kernel, grid_spec=pltpu.PrefetchScalarGridSpec(num_scalar_...  86.8 us
    ppermute x21, starting transfers between devices, swap(): return lax.ppermute(v, 'col', [(i, i ^ bit) for i in range(n)])  50.5 us
    pallas_call x8, Pallas kernels, assemble(): pl.pallas_call(kernel, grid_spec=pltpu.PrefetchScalarGridSpec(num_scalar_...  35.6 us
  transfers between devices with their start and end apart: 25, of which 10 were waited for; matrix products, arithmetic and copies ran while one was open for 0% of the time, Pallas kernels for 24%

profile of v2, /device:TPU:0, one launch (start us, length us, event | category | flops | bytes accessed | tf_op | source)
XLA Modules:
  0.0 402.7 jit_solution(12161447622950824913)
XLA Ops:
  6.5 7.5 %assemble.8 = (bf16[4,128,1024]{2,1,0:T(8,128)(2,1)}, bf16[4,128,1024]{2,1,0:T(8,128)(2,1)}, bf16[8,128,3328]{2,1,0:T(8,128)(2,1)}) custom-call(s32[1]{0:T(128)} %bitcast.m, bf16[128,53248]{1,0:T(8,128)(2,1)} %refs_12_.9, bf16[128,53248]{1,0:T(8,128)(2,1)} %refs_12_.9, bf16[128,53248]{1,0:T(8,128)(2,1)} %refs_12_.9, bf16[128,53248]{1,0:T(8,128)(2,1)} %refs_12_.9, ...), custom_call_target="tpu_custom_call" | custom-call | flops 1 | bytes 1 | tf_op jit(solution)/shard_map/assemble/pallas_call | solution.py:64
  20.6 2.6 collective-permute-start
  25.4 3.8 assemble.10
  29.2 12.1 %collective-permute-done.3.refs_2_.refs_6_.refs_10_.refs_14_ = bf16[4,128,1024]{2,1,0:T(8,128)(2,1)S(1)} collective-permute-done((bf16[4,128,1024]{2,1,0:T(8,128)(2,1)}, bf16[4,128,1024]{2,1,0:T(8,128)(2,1)S(1)}, u32[]{:S(2)}, u32[]{:S(2)}) %collective-permute-start.3) | collective-permute-done | bytes 1048608 | tf_op jit(solution)/shard_map/ppermute | solution.py:146
  41.3 21.9 %collective-permute-done.4.refs_3_.refs_7_.refs_11_.refs_15_ = bf16[4,128,1024]{2,1,0:T(8,128)(2,1)S(1)} collective-permute-done((bf16[4,128,1024]{2,1,0:T(8,128)(2,1)}, bf16[4,128,1024]{2,1,0:T(8,128)(2,1)S(1)}, u32[]{:S(2)}, u32[]{:S(2)}) %collective-permute-start.4) | collective-permute-done | bytes 1048608 | tf_op jit(solution)/shard_map/ppermute | solution.py:146
  64.3 4.7 %assemble.9 = (bf16[4,128,1024]{2,1,0:T(8,128)(2,1)}, bf16[4,128,1024]{2,1,0:T(8,128)(2,1)}, bf16[4,128,1024]{2,1,0:T(8,128)(2,1)}, bf16[4,128,1024]{2,1,0:T(8,128)(2,1)}) custom-call(s32[1]{0:T(128)} %bitcast.m, bf16[128,53248]{1,0:T(8,128)(2,1)} %refs_12_.9, bf16[8,128,3328]{2,1,0:T(8,128)(2,1)} %collective-permute-done.2.refs_1_.refs_5_.refs_9_.refs_13_.refs_3_.refs_7_, ...), custom_call_target="tpu_custom_call" | custom-call | flops 1 | bytes 1 | tf_op jit(solution)/shard_map/assemble/pallas_call | solution.py:64
  77.3 3.8 assemble.12
  81.1 62.8 %collective-permute-done.6.refs_2_.refs_3_.refs_6_.refs_7_.refs_10_.refs_11_.refs_14_.refs_15_ = bf16[8,128,1024]{2,1,0:T(8,128)(2,1)S(1)} collective-permute-done((bf16[8,128,1024]{2,1,0:T(8,128)(2,1)}, bf16[8,128,1024]{2,1,0:T(8,128)(2,1)S(1)}, u32[]{:S(2)}, u32[]{:S(2)}) %collective-permute-start.6) | collective-permute-done | bytes 2097184 | tf_op jit(solution)/shard_map/ppermute | solution.py:146
  145.2 4.7 %assemble.11 = (bf16[4,128,1024]{2,1,0:T(8,128)(2,1)}, bf16[4,128,1024]{2,1,0:T(8,128)(2,1)}, bf16[4,128,1024]{2,1,0:T(8,128)(2,1)}, bf16[4,128,1024]{2,1,0:T(8,128)(2,1)}) custom-call(s32[1]{0:T(128)} %bitcast.m, bf16[128,53248]{1,0:T(8,128)(2,1)} %refs_12_.9, bf16[8,128,3328]{2,1,0:T(8,128)(2,1)} %collective-permute-done.2.refs_1_.refs_5_.refs_9_.refs_13_.refs_3_.refs_7_, ...), custom_call_target="tpu_custom_call" | custom-call | flops 1 | bytes 1 | tf_op jit(solution)/shard_map/assemble/pallas_call | solution.py:64
  150.0 15.4 %collective-permute-done.5 = bf16[128,4096]{1,0:T(8,128)(2,1)} collective-permute-done((bf16[128,4096]{1,0:T(8,128)(2,1)}, bf16[128,4096]{1,0:T(8,128)(2,1)}, u32[]{:S(2)}, u32[]{:S(2)}) %collective-permute-start.5) | collective-permute-done | bytes 1048608 | tf_op jit(solution)/shard_map/ppermute | solution.py:146
  165.9 3.1 collective-permute-start.11
  171.4 3.2 assemble.14
  174.6 49.0 %collective-permute-done.10.refs_2_.refs_3_.refs_6_.refs_7_.refs_10_.refs_11_.refs_14_.refs_15_ = bf16[8,128,768]{2,1,0:T(8,128)(2,1)S(1)} collective-permute-done((bf16[8,128,768]{2,1,0:T(8,128)(2,1)S(1)}, bf16[8,128,768]{2,1,0:T(8,128)(2,1)S(1)}, u32[]{:S(2)}, u32[]{:S(2)}) %collective-permute-start.10) | collective-permute-done | bytes 1572896 | tf_op jit(solution)/shard_map/ppermute | solution.py:146
  224.8 4.3 %assemble.13 = (bf16[4,128,768]{2,1,0:T(8,128)(2,1)}, bf16[4,128,768]{2,1,0:T(8,128)(2,1)}, bf16[4,128,768]{2,1,0:T(8,128)(2,1)}, bf16[4,128,768]{2,1,0:T(8,128)(2,1)}) custom-call(s32[1]{0:T(128)} %bitcast.m, bf16[128,53248]{1,0:T(8,128)(2,1)} %refs_12_.9, bf16[8,128,3328]{2,1,0:T(8,128)(2,1)} %collective-permute-done.2.refs_1_.refs_5_.refs_9_.refs_13_.refs_3_.refs_7_, ...), custom_call_target="tpu_custom_call" | custom-call | flops 1 | bytes 1 | tf_op jit(solution)/shard_map/assemble/pallas_call | solution.py:64
  229.1 12.0 %collective-permute-done.12.refs_6_ = bf16[4,128,1024]{2,1,0:T(8,128)(2,1)S(1)} collective-permute-done((bf16[4,128,1024]{2,1,0:T(8,128)(2,1)}, bf16[4,128,1024]{2,1,0:T(8,128)(2,1)S(1)}, u32[]{:S(2)}, u32[]{:S(2)}) %collective-permute-start.12) | collective-permute-done | bytes 1048608 | tf_op jit(solution)/shard_map/ppermute | solution.py:146
  242.7 20.7 %collective-permute-start.15 = (bf16[4,128,768]{2,1,0:T(8,128)(2,1)}, bf16[4,128,768]{2,1,0:T(8,128)(2,1)S(1)}, u32[]{:S(2)}, u32[]{:S(2)}) collective-permute-start(bf16[4,128,768]{2,1,0:T(8,128)(2,1)} %get-tuple-element.151), channel_id=1, source_target_pairs={{0,4},{1,5},{2,6},{3,7},{4,0},{5,1},{6,2},{7,3},{8,12},{9,13},{10,... | collective-permute-start | bytes 2359304 | tf_op jit(solution)/shard_map/ppermute | solution.py:146
  265.9 16.0 %collective-permute-done.14.refs_2_.refs_3_.refs_6_.refs_7_.refs_10_.refs_11_.refs_14_.refs_15_ = bf16[8,128,512]{2,1,0:T(8,128)(2,1)S(1)} collective-permute-done((bf16[8,128,512]{2,1,0:T(8,128)(2,1)S(1)}, bf16[8,128,512]{2,1,0:T(8,128)(2,1)S(1)}, u32[]{:S(2)}, u32[]{:S(2)}) %collective-permute-start.14) | collective-permute-done | bytes 1048608 | tf_op jit(solution)/shard_map/ppermute | solution.py:146
  282.8 3.7 assemble.15
  286.7 24.6 %merge.4.refs_9_ = bf16[4096,3328]{1,0:T(8,128)(2,1)} custom-call(s32[1]{0:T(128)} %bitcast.m, bf16[512,4096]{1,0:T(8,128)(2,1)} %all-gather.5.cloned.1.call-done.refs_0_, bf16[512,4096]{1,0:T(8,128)(2,1)} %all-gather.7.cloned.1.call-done.refs_1_, bf16[512,4096]{1,0:T(8,128)(2,1)} %all-gather.9.cloned.1.call-done.refs_2_, ...), custom_call_target="tpu_custom_call" | custom-call | flops 1 | bytes 1 | tf_op jit(solution)/shard_map/merge/pallas_call | solution.py:122
  311.3 25.0 %merge.5.refs_9_ = bf16[4096,3328]{1,0:T(8,128)(2,1)} custom-call(s32[1]{0:T(128)} %bitcast.m, bf16[512,4096]{1,0:T(8,128)(2,1)} %all-gather.5.cloned.1.call-done.refs_0_, bf16[512,4096]{1,0:T(8,128)(2,1)} %all-gather.7.cloned.1.call-done.refs_1_, bf16[512,4096]{1,0:T(8,128)(2,1)} %all-gather.9.cloned.1.call-done.refs_2_, ...), custom_call_target="tpu_custom_call", output_to_operand_aliasing={{}: (10, {})} | custom-call | flops 1 | bytes 1 | tf_op jit(solution)/shard_map/merge/pallas_call | solution.py:122
  336.4 3.2 collective-permute-start.18
  342.1 20.5 %merge.6.refs_9_ = bf16[4096,3328]{1,0:T(8,128)(2,1)} custom-call(s32[1]{0:T(128)} %bitcast.m, bf16[512,4096]{1,0:T(8,128)(2,1)} %all-gather.5.cloned.1.call-done.refs_0_, bf16[512,4096]{1,0:T(8,128)(2,1)} %all-gather.7.cloned.1.call-done.refs_1_, bf16[512,4096]{1,0:T(8,128)(2,1)} %all-gather.9.cloned.1.call-done.refs_2_, ...), custom_call_target="tpu_custom_call", output_to_operand_aliasing={{}: (10, {})} | custom-call | flops 1 | bytes 1 | tf_op jit(solution)/shard_map/merge/pallas_call | solution.py:122
  362.6 15.2 %collective-permute-done.19.refs_6_ = bf16[4,128,512]{2,1,0:T(8,128)(2,1)S(1)} collective-permute-done((bf16[4,128,512]{2,1,0:T(8,128)(2,1)S(1)}, bf16[4,128,512]{2,1,0:T(8,128)(2,1)S(1)}, u32[]{:S(2)}, u32[]{:S(2)}) %collective-permute-start.19) | collective-permute-done | bytes 524320 | tf_op jit(solution)/shard_map/ppermute | solution.py:146
  379.4 16.7 %merge.7 = bf16[4096,3328]{1,0:T(8,128)(2,1)} custom-call(s32[1]{0:T(128)} %bitcast.m, bf16[512,4096]{1,0:T(8,128)(2,1)} %all-gather.5.cloned.1.call-done.refs_0_, bf16[512,4096]{1,0:T(8,128)(2,1)} %all-gather.7.cloned.1.call-done.refs_1_, bf16[512,4096]{1,0:T(8,128)(2,1)} %all-gather.9.cloned.1.call-done.refs_2_, ...), custom_call_target="tpu_custom_call", output_to_operand_aliasing={{}: (10, {})} | custom-call | flops 1 | bytes 1 | tf_op jit(solution)/shard_map/merge/pallas_call | solution.py:122
  (89 shorter events, 32.8 us)
Async XLA Ops:
  6.5 280.1 %all-gather.5.cloned.1.call-start = ((), (), s32[]{:S(2)}) async-start(), calls=%async_computation | async-start | bytes 5242880 | tf_op jit(solution)/shard_map/all_gather | solution.py:165
  14.5 26.8 %collective-permute-start.3 = (bf16[4,128,1024]{2,1,0:T(8,128)(2,1)}, bf16[4,128,1024]{2,1,0:T(8,128)(2,1)S(1)}, u32[]{:S(2)}, u32[]{:S(2)}) collective-permute-start(bf16[4,128,1024]{2,1,0:T(8,128)(2,1)} %get-tuple-element.85), channel_id=1, source_target_pairs={{0,2},{1,3},{2,0},{3,1},{4,6},{5,7},{6,4},{7,5},{8,10},{9,11},{10,... | collective-permute-start | bytes 3145736 | tf_op jit(solution)/shard_map/ppermute | solution.py:146
  17.1 46.2 %collective-permute-start.4 = (bf16[4,128,1024]{2,1,0:T(8,128)(2,1)}, bf16[4,128,1024]{2,1,0:T(8,128)(2,1)S(1)}, u32[]{:S(2)}, u32[]{:S(2)}) collective-permute-start(bf16[4,128,1024]{2,1,0:T(8,128)(2,1)} %get-tuple-element.86), channel_id=1, source_target_pairs={{0,3},{1,2},{2,1},{3,0},{4,7},{5,6},{6,5},{7,4},{8,11},{9,10},{10,... | collective-permute-start | bytes 3145736 | tf_op jit(solution)/shard_map/ppermute | solution.py:146
  18.8 50.3 %collective-permute-start.1 = (bf16[128,4096]{1,0:T(8,128)(2,1)S(1)}, bf16[128,4096]{1,0:T(8,128)(2,1)}, u32[]{:S(2)}, u32[]{:S(2)}) collective-permute-start(bf16[128,4096]{1,0:T(8,128)(2,1)S(1)} %multiply_convert_fusion), channel_id=1, source_target_pairs={{0,4},{1,5},{2,6},{3,7},{4,0},{5,1},{6,2},{7,3},{8,12},{9,13},{10,... | collective-permute-start | bytes 3145736 | tf_op jit(solution)/shard_map/ppermute | solution.py:146
  20.6 48.6 %collective-permute-start = (bf16[128,4096]{1,0:T(8,128)(2,1)S(1)}, bf16[128,4096]{1,0:T(8,128)(2,1)}, u32[]{:S(2)}, u32[]{:S(2)}) collective-permute-start(bf16[128,4096]{1,0:T(8,128)(2,1)S(1)} %multiply_convert_fusion), channel_id=1, source_target_pairs={{0,8},{1,9},{2,10},{3,11},{4,12},{5,13},{6,14},{7,15},{8,0},{9,1},... | collective-permute-start | bytes 3145736 | tf_op jit(solution)/shard_map/ppermute | solution.py:146
  69.3 217.3 %all-gather.7.cloned.1.call-start = ((), (), s32[]{:S(2)}) async-start(), calls=%async_computation.1 | async-start | bytes 5242880 | tf_op jit(solution)/shard_map/all_gather | solution.py:165
  70.1 216.6 %all-gather.9.cloned.1.call-start = ((), (), s32[]{:S(2)}) async-start(), calls=%async_computation.2 | async-start | bytes 5242880 | tf_op jit(solution)/shard_map/all_gather | solution.py:165
  70.8 215.9 %all-gather.11.cloned.1.call-start = ((), (), s32[]{:S(2)}) async-start(), calls=%async_computation.3 | async-start | bytes 5242880 | tf_op jit(solution)/shard_map/all_gather | solution.py:165
  70.8 73.0 %collective-permute-start.6 = (bf16[8,128,1024]{2,1,0:T(8,128)(2,1)}, bf16[8,128,1024]{2,1,0:T(8,128)(2,1)S(1)}, u32[]{:S(2)}, u32[]{:S(2)}) collective-permute-start(bf16[8,128,1024]{2,1,0:T(8,128)(2,1)} %assemble.10), channel_id=1, source_target_pairs={{0,2},{1,3},{2,0},{3,1},{4,6},{5,7},{6,4},{7,5},{8,10},{9,11},{10,... | collective-permute-start | bytes 6291464 | tf_op jit(solution)/shard_map/ppermute | solution.py:146
  72.4 77.5 %collective-permute-start.7 = (bf16[4,128,1024]{2,1,0:T(8,128)(2,1)}, bf16[4,128,1024]{2,1,0:T(8,128)(2,1)S(1)}, u32[]{:S(2)}, u32[]{:S(2)}) collective-permute-start(bf16[4,128,1024]{2,1,0:T(8,128)(2,1)} %get-tuple-element.100), channel_id=1, source_target_pairs={{0,4},{1,5},{2,6},{3,7},{4,0},{5,1},{6,2},{7,3},{8,12},{9,13},{10,... | collective-permute-start | bytes 3145736 | tf_op jit(solution)/shard_map/ppermute | solution.py:146
  73.8 76.2 %collective-permute-start.8 = (bf16[4,128,1024]{2,1,0:T(8,128)(2,1)}, bf16[4,128,1024]{2,1,0:T(8,128)(2,1)}, u32[]{:S(2)}, u32[]{:S(2)}) collective-permute-start(bf16[4,128,1024]{2,1,0:T(8,128)(2,1)} %get-tuple-element.101), channel_id=1, source_target_pairs={{0,8},{1,9},{2,10},{3,11},{4,12},{5,13},{6,14},{7,15},{8,0},{9,1},... | collective-permute-start | bytes 3145736 | tf_op jit(solution)/shard_map/ppermute | solution.py:146
  76.4 73.6 %collective-permute-start.9 = (bf16[4,128,1024]{2,1,0:T(8,128)(2,1)}, bf16[4,128,1024]{2,1,0:T(8,128)(2,1)}, u32[]{:S(2)}, u32[]{:S(2)}) collective-permute-start(bf16[4,128,1024]{2,1,0:T(8,128)(2,1)} %get-tuple-element.102), channel_id=1, source_target_pairs={{0,12},{1,13},{2,14},{3,15},{4,8},{5,9},{6,10},{7,11},{8,4},{9,5},... | collective-permute-start | bytes 3145736 | tf_op jit(solution)/shard_map/ppermute | solution.py:146
  76.8 88.6 %collective-permute-start.5 = (bf16[128,4096]{1,0:T(8,128)(2,1)}, bf16[128,4096]{1,0:T(8,128)(2,1)}, u32[]{:S(2)}, u32[]{:S(2)}) collective-permute-start(bf16[128,4096]{1,0:T(8,128)(2,1)} %collective-permute-done), channel_id=1, source_target_pairs={{0,4},{1,5},{2,6},{3,7},{4,0},{5,1},{6,2},{7,3},{8,12},{9,13},{10,... | collective-permute-start | bytes 3145736 | tf_op jit(solution)/shard_map/ppermute | solution.py:146
  165.4 58.2 %collective-permute-start.10 = (bf16[8,128,768]{2,1,0:T(8,128)(2,1)S(1)}, bf16[8,128,768]{2,1,0:T(8,128)(2,1)S(1)}, u32[]{:S(2)}, u32[]{:S(2)}) collective-permute-start(bf16[8,128,768]{2,1,0:T(8,128)(2,1)S(1)} %copy-done.6), channel_id=1, source_target_pairs={{0,2},{1,3},{2,0},{3,1},{4,6},{5,7},{6,4},{7,5},{8,10},{9,11},{10,... | collective-permute-start | bytes 4718600 | tf_op jit(solution)/shard_map/ppermute | solution.py:146
  165.9 63.2 %collective-permute-start.11 = (bf16[4,128,1024]{2,1,0:T(8,128)(2,1)}, bf16[4,128,1024]{2,1,0:T(8,128)(2,1)S(1)}, u32[]{:S(2)}, u32[]{:S(2)}) collective-permute-start(bf16[4,128,1024]{2,1,0:T(8,128)(2,1)} %get-tuple-element.122), channel_id=1, source_target_pairs={{0,4},{1,5},{2,6},{3,7},{4,0},{5,1},{6,2},{7,3},{8,12},{9,13},{10,... | collective-permute-start | bytes 3145736 | tf_op jit(solution)/shard_map/ppermute | solution.py:146
  168.9 72.1 %collective-permute-start.12 = (bf16[4,128,1024]{2,1,0:T(8,128)(2,1)}, bf16[4,128,1024]{2,1,0:T(8,128)(2,1)S(1)}, u32[]{:S(2)}, u32[]{:S(2)}) collective-permute-start(bf16[4,128,1024]{2,1,0:T(8,128)(2,1)} %get-tuple-element.123), channel_id=1, source_target_pairs={{0,8},{1,9},{2,10},{3,11},{4,12},{5,13},{6,14},{7,15},{8,0},{9,1},... | collective-permute-start | bytes 3145736 | tf_op jit(solution)/shard_map/ppermute | solution.py:146
  170.2 70.8 %collective-permute-start.13 = (bf16[4,128,1024]{2,1,0:T(8,128)(2,1)}, bf16[4,128,1024]{2,1,0:T(8,128)(2,1)S(1)}, u32[]{:S(2)}, u32[]{:S(2)}) collective-permute-start(bf16[4,128,1024]{2,1,0:T(8,128)(2,1)} %get-tuple-element.124), channel_id=1, source_target_pairs={{0,12},{1,13},{2,14},{3,15},{4,8},{5,9},{6,10},{7,11},{8,4},{9,5},... | collective-permute-start | bytes 3145736 | tf_op jit(solution)/shard_map/ppermute | solution.py:146
  241.1 40.8 %collective-permute-start.14 = (bf16[8,128,512]{2,1,0:T(8,128)(2,1)S(1)}, bf16[8,128,512]{2,1,0:T(8,128)(2,1)S(1)}, u32[]{:S(2)}, u32[]{:S(2)}) collective-permute-start(bf16[8,128,512]{2,1,0:T(8,128)(2,1)S(1)} %copy-done.11), channel_id=1, source_target_pairs={{0,2},{1,3},{2,0},{3,1},{4,6},{5,7},{6,4},{7,5},{8,10},{9,11},{10,... | collective-permute-start | bytes 3145736 | tf_op jit(solution)/shard_map/ppermute | solution.py:146
  242.7 93.7 %collective-permute-start.15 = (bf16[4,128,768]{2,1,0:T(8,128)(2,1)}, bf16[4,128,768]{2,1,0:T(8,128)(2,1)S(1)}, u32[]{:S(2)}, u32[]{:S(2)}) collective-permute-start(bf16[4,128,768]{2,1,0:T(8,128)(2,1)} %get-tuple-element.151), channel_id=1, source_target_pairs={{0,4},{1,5},{2,6},{3,7},{4,0},{5,1},{6,2},{7,3},{8,12},{9,13},{10,... | collective-permute-start | bytes 2359304 | tf_op jit(solution)/shard_map/ppermute | solution.py:146
  263.4 72.9 %collective-permute-start.16 = (bf16[4,128,768]{2,1,0:T(8,128)(2,1)}, bf16[4,128,768]{2,1,0:T(8,128)(2,1)S(1)}, u32[]{:S(2)}, u32[]{:S(2)}) collective-permute-start(bf16[4,128,768]{2,1,0:T(8,128)(2,1)} %get-tuple-element.152), channel_id=1, source_target_pairs={{0,8},{1,9},{2,10},{3,11},{4,12},{5,13},{6,14},{7,15},{8,0},{9,1},... | collective-permute-start | bytes 2359304 | tf_op jit(solution)/shard_map/ppermute | solution.py:146
  264.4 72.0 %collective-permute-start.17 = (bf16[4,128,768]{2,1,0:T(8,128)(2,1)}, bf16[4,128,768]{2,1,0:T(8,128)(2,1)S(1)}, u32[]{:S(2)}, u32[]{:S(2)}) collective-permute-start(bf16[4,128,768]{2,1,0:T(8,128)(2,1)} %get-tuple-element.153), channel_id=1, source_target_pairs={{0,12},{1,13},{2,14},{3,15},{4,8},{5,9},{6,10},{7,11},{8,4},{9,5},... | collective-permute-start | bytes 2359304 | tf_op jit(solution)/shard_map/ppermute | solution.py:146
  336.4 26.2 %collective-permute-start.18 = (bf16[4,128,512]{2,1,0:T(8,128)(2,1)S(1)}, bf16[4,128,512]{2,1,0:T(8,128)(2,1)S(1)}, u32[]{:S(2)}, u32[]{:S(2)}) collective-permute-start(bf16[4,128,512]{2,1,0:T(8,128)(2,1)S(1)} %copy-done.20), channel_id=1, source_target_pairs={{0,4},{1,5},{2,6},{3,7},{4,0},{5,1},{6,2},{7,3},{8,12},{9,13},{10,... | collective-permute-start | bytes 1572872 | tf_op jit(solution)/shard_map/ppermute | solution.py:146
  339.5 38.2 %collective-permute-start.19 = (bf16[4,128,512]{2,1,0:T(8,128)(2,1)S(1)}, bf16[4,128,512]{2,1,0:T(8,128)(2,1)S(1)}, u32[]{:S(2)}, u32[]{:S(2)}) collective-permute-start(bf16[4,128,512]{2,1,0:T(8,128)(2,1)S(1)} %copy-done.19), channel_id=1, source_target_pairs={{0,8},{1,9},{2,10},{3,11},{4,12},{5,13},{6,14},{7,15},{8,0},{9,1},... | collective-permute-start | bytes 1572872 | tf_op jit(solution)/shard_map/ppermute | solution.py:146
  340.6 37.1 %collective-permute-start.20 = (bf16[4,128,512]{2,1,0:T(8,128)(2,1)S(1)}, bf16[4,128,512]{2,1,0:T(8,128)(2,1)S(1)}, u32[]{:S(2)}, u32[]{:S(2)}) collective-permute-start(bf16[4,128,512]{2,1,0:T(8,128)(2,1)S(1)} %copy-done.18), channel_id=1, source_target_pairs={{0,12},{1,13},{2,14},{3,15},{4,8},{5,9},{6,10},{7,11},{8,4},{9,5},... | collective-permute-start | bytes 1572872 | tf_op jit(solution)/shard_map/ppermute | solution.py:146
  (23 other events, 435.3 us)
Sparse Core Ops, SparseCore 0:
  69.4 58.4 all-gather.4
  129.5 35.9 all-gather.6
  167.0 57.5 all-gather.8
  226.1 53.3 all-gather.10

commit v3 on v2

--- a/solution.py
+++ b/solution.py
@@ -7,8 +7,9 @@
 from jax.sharding import PartitionSpec as P
 
 RANK = 64
-UNIT = 256
-ORDER = (0, 1, 2, 3, 0, 1, 2, 3, 0, 1, 2, 0, 1)
+UNIT = 128
+TILE = 1024
+SHARES = (7, 8, 8, 3)
 VMEM = 56 * 1024 * 1024
 NO_COST = pl.CostEstimate(flops=1, bytes_accessed=1, transcendentals=0)
 ANY = pl.BlockSpec(memory_space=pl.ANY)
@@ -16,12 +17,10 @@
 
 def chunk_spans(width):
     units = width // UNIT
-    if width % UNIT or units < 8:
+    if width % UNIT or units < sum(SHARES):
         return [(0, width)]
-    sizes = [0, 0, 0, 0]
-    for i in range(units):
-        sizes[ORDER[i % len(ORDER)]] += UNIT
-    return [(sum(sizes[:i]), s) for i, s in enumerate(sizes)]
+    ends = [units * sum(SHARES[: i + 1]) // sum(SHARES) * UNIT for i in range(len(SHARES))]
+    return [(start, end - start) for start, end in zip([0] + ends, ends)]
 
 
 def assemble(plan, sources, me, depth, width):
@@ -78,42 +77,29 @@
 
 def merge(lefts, rights, me, base, out, offset, w):
     rows, width = base.shape
-    depth = rights[0].shape[1]
-    tile, near, groups = 512, rights[0].shape[0], len(lefts)
-    n = near * groups
+    near, depth, _ = rights[0].shape
+    groups, tile = len(lefts), TILE
     if w == width:
         slab = pl.BlockSpec((tile, w), lambda i, m: (i, 0))
     else:
         slab = pl.BlockSpec((pl.Element(tile), pl.Element(w)), lambda i, m: (i * tile, offset))
 
     def kernel(m, *refs):
-        left, right = refs[:groups], refs[groups : 2 * groups]
-        base_ref, (out_ref, panel, sem) = refs[2 * groups], refs[-3:]
-
-        @pl.when(pl.program_id(0) == 0)
-        def _():
-            copies = []
-            for g in range(groups):
-                for j in range(near):
-                    place = g * near + (m[0] ^ j) % near
-                    copies.append(pltpu.make_async_copy(right[g].at[j], panel.at[place], sem.at[g * near + j]))
-            for c in copies:
-                c.start()
-            for c in copies:
-                c.wait()
-
+        left, right = refs[:groups], refs[groups : groups * (1 + near)]
+        base_ref, out_ref = refs[groups * (1 + near)], refs[-1]
         update = 0.0
         for g in range(groups):
+            panel = jnp.concatenate([r[0] for r in right[g * near : (g + 1) * near]], axis=0)
             update += lax.dot_general(
-                left[g][...],
-                panel[g * near : (g + 1) * near].reshape(near * depth, w),
-                (((0,), (0,)), ((), ())),
-                preferred_element_type=jnp.float32,
+                left[g][...], panel, (((0,), (0,)), ((), ())), preferred_element_type=jnp.float32
             )
         out_ref[...] = (base_ref[...].astype(jnp.float32) + update).astype(out_ref.dtype)
 
-    in_specs = [pl.BlockSpec((near * depth, tile), lambda i, m: (0, i))] * groups + [ANY] * groups + [slab]
-    operands = [*lefts, *rights, base]
+    blocks = [
+        pl.BlockSpec((1, depth, w), lambda i, m, j=j: ((m[0] ^ j) % near, 0, 0)) for j in range(near)
+    ]
+    in_specs = [pl.BlockSpec((near * depth, tile), lambda i, m: (0, i))] * groups + blocks * groups + [slab]
+    operands = [*lefts, *[r for r in rights for _ in range(near)], base]
     aliases = {}
     if out is not None:
         in_specs.append(ANY)
@@ -122,11 +108,7 @@
     return pl.pallas_call(
         kernel,
         grid_spec=pltpu.PrefetchScalarGridSpec(
-            num_scalar_prefetch=1,
-            grid=(rows // tile,),
-            in_specs=in_specs,
-            out_specs=slab,
-            scratch_shapes=[pltpu.VMEM((n, depth, w), base.dtype), pltpu.SemaphoreType.DMA((n,))],
+            num_scalar_prefetch=1, grid=(rows // tile,), in_specs=in_specs, out_specs=slab
         ),
         out_shape=jax.ShapeDtypeStruct(base.shape, base.dtype),
         input_output_aliases=aliases,
@@ -170,10 +152,10 @@
     put = functools.partial(assemble, me=me, depth=depth, width=width)
 
     to_core = [("own", 4 * dz + 2 * dx + 1) for dx in range(2) for dz in range(quads)]
-    to_2, to_3, to_1 = put(
-        [(0, w0, [("own", 4 * dz + j) for dz in range(quads)]) for j in (2, 3)] + [(0, width, to_core)],
-        {"up": up_factors},
+    to_2, to_3 = put(
+        [(0, w0, [("own", 4 * dz + j) for dz in range(quads)]) for j in (2, 3)], {"up": up_factors}
     )
+    to_1 = put([(0, width, to_core)], {"up": up_factors})[0]
     got_2, got_3, got_c = swap(to_2, 2), swap(to_3, 3), swap(to_1, 1)
     src = {"up": up_factors, "core": got_c, 2: got_2, 3: got_3}
 
@@ -189,6 +171,9 @@
             for dz in range(quads)
         ], {**src, "x": got_x})
 
+    far, held, got_2, got_3 = lax.optimization_barrier((far, held, got_2, got_3))
+    lefts = {half: gather(far)}
+    src.update({2: got_2, 3: got_3})
     to_x = for_x(1) if last else None
     to_z = put([
         (0, w0, [("own", 4 * dz), ("core", dz, 0), (2, dz, 0), (3, dz, 0)]) for dz in range(quads)
@@ -196,8 +181,7 @@
 
     out, panels, merged = None, [], 0
     far, held, to_z, to_x = lax.optimization_barrier((far, held, to_z, to_x))
-    lefts = {k: gather(v) for k, v in held.items()}
-    lefts[half] = gather(far)
+    lefts.update({k: gather(v) for k, v in held.items()})
     far_held = across(far, half)
     for q in range(last + 1):
         if q:

time: 409 us -> 397 us (0.971)
  waiting for transfers between devices: 208 us -> 190 us
  starting transfers between devices: 50.6 us -> 55.7 us
    ppermute x21, waiting for transfers between devices: 207 us -> 189 us  [swap(): return lax.ppermute(v, 'col', [(i, i ^ bit) for i in range(n)])]
    ppermute x21, starting transfers between devices: 50.5 us -> 55.6 us  [swap(): return lax.ppermute(v, 'col', [(i, i ^ bit) for i in range(n)])]
    pallas_call x8 -> x9, Pallas kernels: 35.6 us -> 38.6 us  [assemble(): pl.pallas_call(kernel, grid_spec=pltpu.PrefetchScalarGridSpec(num_scalar_...]
  transfers between devices with their start and end apart: 25 -> 25, of which waited for: 10 -> 8; matrix products, arithmetic and copies ran while one was open for 0% -> 0% of each run, Pallas kernels for 24% -> 28%
where the time goes in v3:
time: 397 us; the launch traced here: 393 us
  waiting for transfers between devices  190 us (48%)
  Pallas kernels  125 us (31%)
  starting transfers between devices  55.7 us (14%)
  between operations  13.4 us (3%)
  local copies, waits for them, and re-layouts  6.08 us (2%)
    ppermute x21, waiting for transfers between devices, swap(): return lax.ppermute(v, 'col', [(i, i ^ bit) for i in range(n)])  189 us
    pallas_call x4, Pallas kernels, merge(): pl.pallas_call(kernel, grid_spec=pltpu.PrefetchScalarGridSpec(num_scalar_...  86.8 us
    ppermute x21, starting transfers between devices, swap(): return lax.ppermute(v, 'col', [(i, i ^ bit) for i in range(n)])  55.6 us
    pallas_call x9, Pallas kernels, assemble(): pl.pallas_call(kernel, grid_spec=pltpu.PrefetchScalarGridSpec(num_scalar_...  38.6 us
  transfers between devices with their start and end apart: 25, of which 8 were waited for; matrix products, arithmetic and copies ran while one was open for 0% of the time, Pallas kernels for 28%

profile of v3, /device:TPU:0, one launch (start us, length us, event | category | flops | bytes accessed | tf_op | source)
XLA Modules:
  0.0 393.0 jit_solution(9779031548633575863)
XLA Ops:
  8.8 3.1 collective-permute-start.1
  11.9 2.6 collective-permute-start
  14.5 3.7 assemble.9
  19.7 6.3 %assemble.10 = bf16[8,128,3328]{2,1,0:T(8,128)(2,1)} custom-call(s32[1]{0:T(128)} %bitcast.m, bf16[128,53248]{1,0:T(8,128)(2,1)} %refs_12_.7, bf16[128,53248]{1,0:T(8,128)(2,1)} %refs_12_.7, bf16[128,53248]{1,0:T(8,128)(2,1)} %refs_12_.7, bf16[128,53248]{1,0:T(8,128)(2,1)} %refs_12_.7, bf16[128,53248]{1,0:T(8,128)(2,1)} %refs_12_.7, ...), custom_call_target="tpu_custom_call" | custom-call | flops 1 | bytes 1 | tf_op jit(solution)/shard_map/assemble/pallas_call | solution.py:63
  26.6 15.2 %collective-permute-done.2.refs_2_.refs_6_.refs_10_.refs_14_ = bf16[4,128,896]{2,1,0:T(8,128)(2,1)S(1)} collective-permute-done((bf16[4,128,896]{2,1,0:T(8,128)(2,1)}, bf16[4,128,896]{2,1,0:T(8,128)(2,1)S(1)}, u32[]{:S(2)}, u32[]{:S(2)}) %collective-permute-start.2) | collective-permute-done | bytes 917536 | tf_op jit(solution)/shard_map/ppermute | solution.py:128
  41.7 17.0 %collective-permute-done.3.refs_3_.refs_7_.refs_11_.refs_15_ = bf16[4,128,896]{2,1,0:T(8,128)(2,1)S(1)} collective-permute-done((bf16[4,128,896]{2,1,0:T(8,128)(2,1)}, bf16[4,128,896]{2,1,0:T(8,128)(2,1)S(1)}, u32[]{:S(2)}, u32[]{:S(2)}) %collective-permute-start.3) | collective-permute-done | bytes 917536 | tf_op jit(solution)/shard_map/ppermute | solution.py:128
  60.1 3.8 assemble.12
  63.9 4.6 %assemble.11 = (bf16[4,128,896]{2,1,0:T(8,128)(2,1)}, bf16[4,128,896]{2,1,0:T(8,128)(2,1)}, bf16[4,128,896]{2,1,0:T(8,128)(2,1)}, bf16[4,128,896]{2,1,0:T(8,128)(2,1)}) custom-call(s32[1]{0:T(128)} %bitcast.m, bf16[128,53248]{1,0:T(8,128)(2,1)} %refs_12_.7, bf16[8,128,3328]{2,1,0:T(8,128)(2,1)} %collective-permute-done.4.refs_1_.refs_5_.refs_9_.refs_13_.refs_3_.refs_7_, ...), custom_call_target="tpu_custom_call" | custom-call | flops 1 | bytes 1 | tf_op jit(solution)/shard_map/assemble/pallas_call | solution.py:63
  75.6 3.8 assemble.14
  79.4 68.2 %collective-permute-done.6.refs_2_.refs_3_.refs_6_.refs_7_.refs_10_.refs_11_.refs_14_.refs_15_ = bf16[8,128,1024]{2,1,0:T(8,128)(2,1)S(1)} collective-permute-done((bf16[8,128,1024]{2,1,0:T(8,128)(2,1)}, bf16[8,128,1024]{2,1,0:T(8,128)(2,1)S(1)}, u32[]{:S(2)}, u32[]{:S(2)}) %collective-permute-start.6) | collective-permute-done | bytes 2097184 | tf_op jit(solution)/shard_map/ppermute | solution.py:128
  149.0 4.7 %assemble.13 = (bf16[4,128,1024]{2,1,0:T(8,128)(2,1)}, bf16[4,128,1024]{2,1,0:T(8,128)(2,1)}, bf16[4,128,1024]{2,1,0:T(8,128)(2,1)}, bf16[4,128,1024]{2,1,0:T(8,128)(2,1)}) custom-call(s32[1]{0:T(128)} %bitcast.m, bf16[128,53248]{1,0:T(8,128)(2,1)} %refs_12_.7, bf16[8,128,3328]{2,1,0:T(8,128)(2,1)} %collective-permute-done.4.refs_1_.refs_5_.refs_9_.refs_13_.refs_3_.refs_7_, ...), custom_call_target="tpu_custom_call" | custom-call | flops 1 | bytes 1 | tf_op jit(solution)/shard_map/assemble/pallas_call | solution.py:63
  156.9 2.4 collective-permute-start.12
  161.0 3.2 assemble.16
  164.2 63.8 %collective-permute-done.10.refs_2_.refs_3_.refs_6_.refs_7_.refs_10_.refs_11_.refs_14_.refs_15_ = bf16[8,128,1024]{2,1,0:T(8,128)(2,1)S(1)} collective-permute-done((bf16[8,128,1024]{2,1,0:T(8,128)(2,1)}, bf16[8,128,1024]{2,1,0:T(8,128)(2,1)S(1)}, u32[]{:S(2)}, u32[]{:S(2)}) %collective-permute-start.10) | collective-permute-done | bytes 2097184 | tf_op jit(solution)/shard_map/ppermute | solution.py:128
  229.3 5.0 %assemble.15 = (bf16[4,128,1024]{2,1,0:T(8,128)(2,1)}, bf16[4,128,1024]{2,1,0:T(8,128)(2,1)}, bf16[4,128,1024]{2,1,0:T(8,128)(2,1)}, bf16[4,128,1024]{2,1,0:T(8,128)(2,1)}) custom-call(s32[1]{0:T(128)} %bitcast.m, bf16[128,53248]{1,0:T(8,128)(2,1)} %refs_12_.7, bf16[8,128,3328]{2,1,0:T(8,128)(2,1)} %collective-permute-done.4.refs_1_.refs_5_.refs_9_.refs_13_.refs_3_.refs_7_, ...), custom_call_target="tpu_custom_call" | custom-call | flops 1 | bytes 1 | tf_op jit(solution)/shard_map/assemble/pallas_call | solution.py:63
  234.4 15.3 %collective-permute-start.15 = (bf16[4,128,1024]{2,1,0:T(8,128)(2,1)}, bf16[4,128,1024]{2,1,0:T(8,128)(2,1)S(1)}, u32[]{:S(2)}, u32[]{:S(2)}) collective-permute-start(bf16[4,128,1024]{2,1,0:T(8,128)(2,1)} %get-tuple-element.159), channel_id=1, source_target_pairs={{0,4},{1,5},{2,6},{3,7},{4,0},{5,1},{6,2},{7,3},{8,12},{9,13},{10,... | collective-permute-start | bytes 3145736 | tf_op jit(solution)/shard_map/ppermute | solution.py:128
  253.7 20.6 %collective-permute-done.14.refs_2_.refs_3_.refs_6_.refs_7_.refs_10_.refs_11_.refs_14_.refs_15_ = bf16[8,128,384]{2,1,0:T(8,128)(2,1)S(1)} collective-permute-done((bf16[8,128,384]{2,1,0:T(8,128)(2,1)S(1)}, bf16[8,128,384]{2,1,0:T(8,128)(2,1)S(1)}, u32[]{:S(2)}, u32[]{:S(2)}) %collective-permute-start.14) | collective-permute-done | bytes 786464 | tf_op jit(solution)/shard_map/ppermute | solution.py:128
  275.2 3.6 assemble.17
  278.9 24.0 %merge.4.refs_21_ = bf16[4096,3328]{1,0:T(8,128)(2,1)} custom-call(s32[1]{0:T(128)} %bitcast.m, bf16[512,4096]{1,0:T(8,128)(2,1)} %all-gather.5.cloned.1.call-done.refs_0_, bf16[512,4096]{1,0:T(8,128)(2,1)} %all-gather.7.cloned.1.call-done.refs_1_, bf16[512,4096]{1,0:T(8,128)(2,1)} %all-gather.9.cloned.1.call-done.refs_2_, ...), custom_call_target="tpu_custom_call" | custom-call | flops 1 | bytes 1 | tf_op jit(solution)/shard_map/merge/pallas_call | solution.py:108
  303.0 24.3 %merge.5.refs_21_ = bf16[4096,3328]{1,0:T(8,128)(2,1)} custom-call(s32[1]{0:T(128)} %bitcast.m, bf16[512,4096]{1,0:T(8,128)(2,1)} %all-gather.5.cloned.1.call-done.refs_0_, bf16[512,4096]{1,0:T(8,128)(2,1)} %all-gather.7.cloned.1.call-done.refs_1_, bf16[512,4096]{1,0:T(8,128)(2,1)} %all-gather.9.cloned.1.call-done.refs_2_, ...), custom_call_target="tpu_custom_call", output_to_operand_aliasing={{}: (22, {})} | custom-call | flops 1 | bytes 1 | tf_op jit(solution)/shard_map/merge/pallas_call | solution.py:108
  327.3 14.1 %collective-permute-start.18 = (bf16[4,128,384]{2,1,0:T(8,128)(2,1)S(1)}, bf16[4,128,384]{2,1,0:T(8,128)(2,1)S(1)}, u32[]{:S(2)}, u32[]{:S(2)}) collective-permute-start(bf16[4,128,384]{2,1,0:T(8,128)(2,1)S(1)} %copy-done.17), channel_id=1, source_target_pairs={{0,4},{1,5},{2,6},{3,7},{4,0},{5,1},{6,2},{7,3},{8,12},{9,13},{10,... | collective-permute-start | bytes 1179656 | tf_op jit(solution)/shard_map/ppermute | solution.py:128
  344.6 24.4 %merge.6.refs_21_ = bf16[4096,3328]{1,0:T(8,128)(2,1)} custom-call(s32[1]{0:T(128)} %bitcast.m, bf16[512,4096]{1,0:T(8,128)(2,1)} %all-gather.5.cloned.1.call-done.refs_0_, bf16[512,4096]{1,0:T(8,128)(2,1)} %all-gather.7.cloned.1.call-done.refs_1_, bf16[512,4096]{1,0:T(8,128)(2,1)} %all-gather.9.cloned.1.call-done.refs_2_, ...), custom_call_target="tpu_custom_call", output_to_operand_aliasing={{}: (22, {})} | custom-call | flops 1 | bytes 1 | tf_op jit(solution)/shard_map/merge/pallas_call | solution.py:108
  369.0 1.9 collective-permute-done.19.refs_12_.refs_13_.refs_14_.refs_15_
  372.4 14.0 %merge.7 = bf16[4096,3328]{1,0:T(8,128)(2,1)} custom-call(s32[1]{0:T(128)} %bitcast.m, bf16[512,4096]{1,0:T(8,128)(2,1)} %all-gather.5.cloned.1.call-done.refs_0_, bf16[512,4096]{1,0:T(8,128)(2,1)} %all-gather.7.cloned.1.call-done.refs_1_, bf16[512,4096]{1,0:T(8,128)(2,1)} %all-gather.9.cloned.1.call-done.refs_2_, ...), custom_call_target="tpu_custom_call", output_to_operand_aliasing={{}: (22, {})} | custom-call | flops 1 | bytes 1 | tf_op jit(solution)/shard_map/merge/pallas_call | solution.py:108
  (82 shorter events, 29.9 us)
Async XLA Ops:
  6.5 272.3 %all-gather.9.cloned.1.call-start = ((), (), s32[]{:S(2)}) async-start(), calls=%async_computation.2 | async-start | bytes 5242880 | tf_op jit(solution)/shard_map/all_gather | solution.py:147
  8.8 50.0 %collective-permute-start.1 = (bf16[128,4096]{1,0:T(8,128)(2,1)S(1)}, bf16[128,4096]{1,0:T(8,128)(2,1)}, u32[]{:S(2)}, u32[]{:S(2)}) collective-permute-start(bf16[128,4096]{1,0:T(8,128)(2,1)S(1)} %multiply_convert_fusion), channel_id=1, source_target_pairs={{0,4},{1,5},{2,6},{3,7},{4,0},{5,1},{6,2},{7,3},{8,12},{9,13},{10,... | collective-permute-start | bytes 3145736 | tf_op jit(solution)/shard_map/ppermute | solution.py:128
  11.9 48.1 %collective-permute-start = (bf16[128,4096]{1,0:T(8,128)(2,1)S(1)}, bf16[128,4096]{1,0:T(8,128)(2,1)}, u32[]{:S(2)}, u32[]{:S(2)}) collective-permute-start(bf16[128,4096]{1,0:T(8,128)(2,1)S(1)} %multiply_convert_fusion), channel_id=1, source_target_pairs={{0,8},{1,9},{2,10},{3,11},{4,12},{5,13},{6,14},{7,15},{8,0},{9,1},... | collective-permute-start | bytes 3145736 | tf_op jit(solution)/shard_map/ppermute | solution.py:128
  18.2 23.6 %collective-permute-start.2 = (bf16[4,128,896]{2,1,0:T(8,128)(2,1)}, bf16[4,128,896]{2,1,0:T(8,128)(2,1)S(1)}, u32[]{:S(2)}, u32[]{:S(2)}) collective-permute-start(bf16[4,128,896]{2,1,0:T(8,128)(2,1)} %get-tuple-element.88), channel_id=1, source_target_pairs={{0,2},{1,3},{2,0},{3,1},{4,6},{5,7},{6,4},{7,5},{8,10},{9,11},{10,... | collective-permute-start | bytes 2752520 | tf_op jit(solution)/shard_map/ppermute | solution.py:128
  19.7 39.0 %collective-permute-start.3 = (bf16[4,128,896]{2,1,0:T(8,128)(2,1)}, bf16[4,128,896]{2,1,0:T(8,128)(2,1)S(1)}, u32[]{:S(2)}, u32[]{:S(2)}) collective-permute-start(bf16[4,128,896]{2,1,0:T(8,128)(2,1)} %get-tuple-element.89), channel_id=1, source_target_pairs={{0,3},{1,2},{2,1},{3,0},{4,7},{5,6},{6,5},{7,4},{8,11},{9,10},{10,... | collective-permute-start | bytes 2752520 | tf_op jit(solution)/shard_map/ppermute | solution.py:128
  26.0 34.1 %collective-permute-start.4 = (bf16[8,128,3328]{2,1,0:T(8,128)(2,1)}, bf16[8,128,3328]{2,1,0:T(8,128)(2,1)}, u32[]{:S(2)}, u32[]{:S(2)}) collective-permute-start(bf16[8,128,3328]{2,1,0:T(8,128)(2,1)} %assemble.10), channel_id=1, source_target_pairs={{0,1},{1,0},{2,3},{3,2},{4,5},{5,4},{6,7},{7,6},{8,9},{9,8},{10,11... | collective-permute-start | bytes 20447240 | tf_op jit(solution)/shard_map/ppermute | solution.py:128
  60.0 218.8 %all-gather.5.cloned.1.call-start = ((), (), s32[]{:S(2)}) async-start(), calls=%async_computation | async-start | bytes 5242880 | tf_op jit(solution)/shard_map/all_gather | solution.py:147
  68.6 210.3 %all-gather.7.cloned.1.call-start = ((), (), s32[]{:S(2)}) async-start(), calls=%async_computation.1 | async-start | bytes 5242880 | tf_op jit(solution)/shard_map/all_gather | solution.py:147
  69.3 209.6 %all-gather.11.cloned.1.call-start = ((), (), s32[]{:S(2)}) async-start(), calls=%async_computation.3 | async-start | bytes 5242880 | tf_op jit(solution)/shard_map/all_gather | solution.py:147
  69.3 78.2 %collective-permute-start.6 = (bf16[8,128,1024]{2,1,0:T(8,128)(2,1)}, bf16[8,128,1024]{2,1,0:T(8,128)(2,1)S(1)}, u32[]{:S(2)}, u32[]{:S(2)}) collective-permute-start(bf16[8,128,1024]{2,1,0:T(8,128)(2,1)} %assemble.12), channel_id=1, source_target_pairs={{0,2},{1,3},{2,0},{3,1},{4,6},{5,7},{6,4},{7,5},{8,10},{9,11},{10,... | collective-permute-start | bytes 6291464 | tf_op jit(solution)/shard_map/ppermute | solution.py:128
  70.9 84.1 %collective-permute-start.5 = (bf16[128,4096]{1,0:T(8,128)(2,1)}, bf16[128,4096]{1,0:T(8,128)(2,1)S(1)}, u32[]{:S(2)}, u32[]{:S(2)}) collective-permute-start(bf16[128,4096]{1,0:T(8,128)(2,1)} %collective-permute-done), channel_id=1, source_target_pairs={{0,4},{1,5},{2,6},{3,7},{4,0},{5,1},{6,2},{7,3},{8,12},{9,13},{10,... | collective-permute-start | bytes 3145736 | tf_op jit(solution)/shard_map/ppermute | solution.py:128
  71.2 83.8 %collective-permute-start.7 = (bf16[4,128,896]{2,1,0:T(8,128)(2,1)}, bf16[4,128,896]{2,1,0:T(8,128)(2,1)}, u32[]{:S(2)}, u32[]{:S(2)}) collective-permute-start(bf16[4,128,896]{2,1,0:T(8,128)(2,1)} %get-tuple-element.108), channel_id=1, source_target_pairs={{0,4},{1,5},{2,6},{3,7},{4,0},{5,1},{6,2},{7,3},{8,12},{9,13},{10,... | collective-permute-start | bytes 2752520 | tf_op jit(solution)/shard_map/ppermute | solution.py:128
  72.9 82.1 %collective-permute-start.8 = (bf16[4,128,896]{2,1,0:T(8,128)(2,1)}, bf16[4,128,896]{2,1,0:T(8,128)(2,1)}, u32[]{:S(2)}, u32[]{:S(2)}) collective-permute-start(bf16[4,128,896]{2,1,0:T(8,128)(2,1)} %get-tuple-element.109), channel_id=1, source_target_pairs={{0,8},{1,9},{2,10},{3,11},{4,12},{5,13},{6,14},{7,15},{8,0},{9,1},... | collective-permute-start | bytes 2752520 | tf_op jit(solution)/shard_map/ppermute | solution.py:128
  73.9 81.1 %collective-permute-start.9 = (bf16[4,128,896]{2,1,0:T(8,128)(2,1)}, bf16[4,128,896]{2,1,0:T(8,128)(2,1)}, u32[]{:S(2)}, u32[]{:S(2)}) collective-permute-start(bf16[4,128,896]{2,1,0:T(8,128)(2,1)} %get-tuple-element.110), channel_id=1, source_target_pairs={{0,12},{1,13},{2,14},{3,15},{4,8},{5,9},{6,10},{7,11},{8,4},{9,5},... | collective-permute-start | bytes 2752520 | tf_op jit(solution)/shard_map/ppermute | solution.py:128
  156.0 72.0 %collective-permute-start.10 = (bf16[8,128,1024]{2,1,0:T(8,128)(2,1)}, bf16[8,128,1024]{2,1,0:T(8,128)(2,1)S(1)}, u32[]{:S(2)}, u32[]{:S(2)}) collective-permute-start(bf16[8,128,1024]{2,1,0:T(8,128)(2,1)} %assemble.14), channel_id=1, source_target_pairs={{0,2},{1,3},{2,0},{3,1},{4,6},{5,7},{6,4},{7,5},{8,10},{9,11},{10,... | collective-permute-start | bytes 6291464 | tf_op jit(solution)/shard_map/ppermute | solution.py:128
  156.6 77.7 %collective-permute-start.11 = (bf16[4,128,1024]{2,1,0:T(8,128)(2,1)}, bf16[4,128,1024]{2,1,0:T(8,128)(2,1)S(1)}, u32[]{:S(2)}, u32[]{:S(2)}) collective-permute-start(bf16[4,128,1024]{2,1,0:T(8,128)(2,1)} %get-tuple-element.130), channel_id=1, source_target_pairs={{0,4},{1,5},{2,6},{3,7},{4,0},{5,1},{6,2},{7,3},{8,12},{9,13},{10,... | collective-permute-start | bytes 3145736 | tf_op jit(solution)/shard_map/ppermute | solution.py:128
  156.9 77.5 %collective-permute-start.12 = (bf16[4,128,1024]{2,1,0:T(8,128)(2,1)}, bf16[4,128,1024]{2,1,0:T(8,128)(2,1)S(1)}, u32[]{:S(2)}, u32[]{:S(2)}) collective-permute-start(bf16[4,128,1024]{2,1,0:T(8,128)(2,1)} %get-tuple-element.131), channel_id=1, source_target_pairs={{0,8},{1,9},{2,10},{3,11},{4,12},{5,13},{6,14},{7,15},{8,0},{9,1},... | collective-permute-start | bytes 3145736 | tf_op jit(solution)/shard_map/ppermute | solution.py:128
  159.3 75.1 %collective-permute-start.13 = (bf16[4,128,1024]{2,1,0:T(8,128)(2,1)}, bf16[4,128,1024]{2,1,0:T(8,128)(2,1)S(1)}, u32[]{:S(2)}, u32[]{:S(2)}) collective-permute-start(bf16[4,128,1024]{2,1,0:T(8,128)(2,1)} %get-tuple-element.132), channel_id=1, source_target_pairs={{0,12},{1,13},{2,14},{3,15},{4,8},{5,9},{6,10},{7,11},{8,4},{9,5},... | collective-permute-start | bytes 3145736 | tf_op jit(solution)/shard_map/ppermute | solution.py:128
  234.4 92.9 %collective-permute-start.15 = (bf16[4,128,1024]{2,1,0:T(8,128)(2,1)}, bf16[4,128,1024]{2,1,0:T(8,128)(2,1)S(1)}, u32[]{:S(2)}, u32[]{:S(2)}) collective-permute-start(bf16[4,128,1024]{2,1,0:T(8,128)(2,1)} %get-tuple-element.159), channel_id=1, source_target_pairs={{0,4},{1,5},{2,6},{3,7},{4,0},{5,1},{6,2},{7,3},{8,12},{9,13},{10,... | collective-permute-start | bytes 3145736 | tf_op jit(solution)/shard_map/ppermute | solution.py:128
  249.6 77.7 %collective-permute-start.16 = (bf16[4,128,1024]{2,1,0:T(8,128)(2,1)}, bf16[4,128,1024]{2,1,0:T(8,128)(2,1)}, u32[]{:S(2)}, u32[]{:S(2)}) collective-permute-start(bf16[4,128,1024]{2,1,0:T(8,128)(2,1)} %get-tuple-element.160), channel_id=1, source_target_pairs={{0,8},{1,9},{2,10},{3,11},{4,12},{5,13},{6,14},{7,15},{8,0},{9,1},... | collective-permute-start | bytes 3145736 | tf_op jit(solution)/shard_map/ppermute | solution.py:128
  250.8 76.5 %collective-permute-start.17 = (bf16[4,128,1024]{2,1,0:T(8,128)(2,1)}, bf16[4,128,1024]{2,1,0:T(8,128)(2,1)}, u32[]{:S(2)}, u32[]{:S(2)}) collective-permute-start(bf16[4,128,1024]{2,1,0:T(8,128)(2,1)} %get-tuple-element.161), channel_id=1, source_target_pairs={{0,12},{1,13},{2,14},{3,15},{4,8},{5,9},{6,10},{7,11},{8,4},{9,5},... | collective-permute-start | bytes 3145736 | tf_op jit(solution)/shard_map/ppermute | solution.py:128
  327.3 41.7 %collective-permute-start.18 = (bf16[4,128,384]{2,1,0:T(8,128)(2,1)S(1)}, bf16[4,128,384]{2,1,0:T(8,128)(2,1)S(1)}, u32[]{:S(2)}, u32[]{:S(2)}) collective-permute-start(bf16[4,128,384]{2,1,0:T(8,128)(2,1)S(1)} %copy-done.17), channel_id=1, source_target_pairs={{0,4},{1,5},{2,6},{3,7},{4,0},{5,1},{6,2},{7,3},{8,12},{9,13},{10,... | collective-permute-start | bytes 1179656 | tf_op jit(solution)/shard_map/ppermute | solution.py:128
  341.5 29.4 %collective-permute-start.19 = (bf16[4,128,384]{2,1,0:T(8,128)(2,1)S(1)}, bf16[4,128,384]{2,1,0:T(8,128)(2,1)S(1)}, u32[]{:S(2)}, u32[]{:S(2)}) collective-permute-start(bf16[4,128,384]{2,1,0:T(8,128)(2,1)S(1)} %copy-done.16), channel_id=1, source_target_pairs={{0,8},{1,9},{2,10},{3,11},{4,12},{5,13},{6,14},{7,15},{8,0},{9,1},... | collective-permute-start | bytes 1179656 | tf_op jit(solution)/shard_map/ppermute | solution.py:128
  343.1 27.8 %collective-permute-start.20 = (bf16[4,128,384]{2,1,0:T(8,128)(2,1)S(1)}, bf16[4,128,384]{2,1,0:T(8,128)(2,1)S(1)}, u32[]{:S(2)}, u32[]{:S(2)}) collective-permute-start(bf16[4,128,384]{2,1,0:T(8,128)(2,1)S(1)} %copy-done.15), channel_id=1, source_target_pairs={{0,12},{1,13},{2,14},{3,15},{4,8},{5,9},{6,10},{7,11},{8,4},{9,5},... | collective-permute-start | bytes 1179656 | tf_op jit(solution)/shard_map/ppermute | solution.py:128
  (19 other events, 403.9 us)
Sparse Core Ops, SparseCore 0:
  60.2 55.5 all-gather.8
  117.3 47.6 all-gather.4
  166.6 56.4 all-gather.6
  224.5 38.5 all-gather.10

commit v4 on v3

--- a/solution.py
+++ b/solution.py
@@ -36,7 +36,7 @@
                     parts.append(sources[b[0]][b[1]][:, b[2] : b[2] + w])
             outs.append(jnp.stack(parts))
         return outs
-    tile = 32 if depth % 32 == 0 else depth
+    tile = 64 if depth % 64 == 0 else depth
     el = pl.Element
     in_specs, operands = [], []
     for offset, w, blocks in plan:
@@ -159,10 +159,10 @@
     got_2, got_3, got_c = swap(to_2, 2), swap(to_3, 3), swap(to_1, 1)
     src = {"up": up_factors, "core": got_c, 2: got_2, 3: got_3}
 
-    def for_x(q):
+    def x_plan(q):
         offset, w = spans[q]
-        plan = [b for dz in range(quads) for b in (("own", 4 * dz + 2), ("core", quads + dz, offset))]
-        return put([(offset, w, plan)], src)[0]
+        return (offset, w, [
+            b for dz in range(quads) for b in (("own", 4 * dz + 2), ("core", quads + dz, offset))])
 
     def for_z(q, got_x):
         offset, w = spans[q]
@@ -174,10 +174,12 @@
     far, held, got_2, got_3 = lax.optimization_barrier((far, held, got_2, got_3))
     lefts = {half: gather(far)}
     src.update({2: got_2, 3: got_3})
-    to_x = for_x(1) if last else None
-    to_z = put([
-        (0, w0, [("own", 4 * dz), ("core", dz, 0), (2, dz, 0), (3, dz, 0)]) for dz in range(quads)
-    ], src)
+    to_z = put(
+        [(0, w0, [("own", 4 * dz), ("core", dz, 0), (2, dz, 0), (3, dz, 0)]) for dz in range(quads)]
+        + ([x_plan(1)] if last else []),
+        src,
+    )
+    to_z, to_x = to_z[:quads], to_z[quads:]
 
     out, panels, merged = None, [], 0
     far, held, to_z, to_x = lax.optimization_barrier((far, held, to_z, to_x))
@@ -191,10 +193,10 @@
             lefts.update({k: gather(v) for k, v in far_held.items() if k != half})
         here = [swap(v, 4 * dz) if dz else v for dz, v in enumerate(to_z)]
         if q < last:
-            got_x = swap(to_x, 2)
+            got_x = swap(to_x[0], 2)
             to_z = for_z(q + 1, got_x)
             if q + 1 < last:
-                to_x = for_x(q + 2)
+                to_x = put([x_plan(q + 2)], src)
         if q == min(2, last):
             lefts, panels = lax.optimization_barrier((lefts, panels))
             left = [lefts[4 * dz] for dz in range(quads)]

time: 397 us -> 388 us (0.977)
  waiting for transfers between devices: 190 us -> 203 us
  Pallas kernels: 125 us -> 114 us
  starting transfers between devices: 55.7 us -> 47.6 us
    ppermute x21, waiting for transfers between devices: 189 us -> 203 us  [swap(): return lax.ppermute(v, 'col', [(i, i ^ bit) for i in range(n)])]
    pallas_call x9 -> x8, Pallas kernels: 38.6 us -> 27.1 us  [assemble(): pl.pallas_call(kernel, grid_spec=pltpu.PrefetchScalarGridSpec(num_scalar_...]
    ppermute x21, starting transfers between devices: 55.6 us -> 47.5 us  [swap(): return lax.ppermute(v, 'col', [(i, i ^ bit) for i in range(n)])]
  transfers between devices with their start and end apart: 25 -> 25, of which waited for: 8 -> 8; matrix products, arithmetic and copies ran while one was open for 0% -> 0% of each run, Pallas kernels for 28% -> 26%
where the time goes in v4:
time: 388 us; the launch traced here: 387 us
  waiting for transfers between devices  203 us (52%)
  Pallas kernels  114 us (29%)
  starting transfers between devices  47.6 us (12%)
  between operations  13.4 us (3%)
  local copies, waits for them, and re-layouts  6.08 us (2%)
    ppermute x21, waiting for transfers between devices, swap(): return lax.ppermute(v, 'col', [(i, i ^ bit) for i in range(n)])  203 us
    pallas_call x4, Pallas kernels, merge(): pl.pallas_call(kernel, grid_spec=pltpu.PrefetchScalarGridSpec(num_scalar_...  86.8 us
    ppermute x21, starting transfers between devices, swap(): return lax.ppermute(v, 'col', [(i, i ^ bit) for i in range(n)])  47.5 us
    pallas_call x8, Pallas kernels, assemble(): pl.pallas_call(kernel, grid_spec=pltpu.PrefetchScalarGridSpec(num_scalar_...  27.1 us
  transfers between devices with their start and end apart: 25, of which 8 were waited for; matrix products, arithmetic and copies ran while one was open for 0% of the time, Pallas kernels for 26%

profile of v4, /device:TPU:0, one launch (start us, length us, event | category | flops | bytes accessed | tf_op | source)
XLA Modules:
  0.0 386.7 jit_solution(15911422887493845628)
XLA Ops:
  8.8 3.1 collective-permute-start.1
  11.9 2.6 collective-permute-start
  14.5 2.6 assemble.8
  18.7 5.1 %assemble.9 = bf16[8,128,3328]{2,1,0:T(8,128)(2,1)} custom-call(s32[1]{0:T(128)} %bitcast.m, bf16[128,53248]{1,0:T(8,128)(2,1)} %refs_12_.7, bf16[128,53248]{1,0:T(8,128)(2,1)} %refs_12_.7, bf16[128,53248]{1,0:T(8,128)(2,1)} %refs_12_.7, bf16[128,53248]{1,0:T(8,128)(2,1)} %refs_12_.7, bf16[128,53248]{1,0:T(8,128)(2,1)} %refs_12_.7, ...), custom_call_target="tpu_custom_call" | custom-call | flops 1 | bytes 1 | tf_op jit(solution)/shard_map/assemble/pallas_call | solution.py:63
  24.3 16.3 %collective-permute-done.2.refs_2_.refs_6_.refs_10_.refs_14_ = bf16[4,128,896]{2,1,0:T(8,128)(2,1)S(1)} collective-permute-done((bf16[4,128,896]{2,1,0:T(8,128)(2,1)}, bf16[4,128,896]{2,1,0:T(8,128)(2,1)S(1)}, u32[]{:S(2)}, u32[]{:S(2)}) %collective-permute-start.2) | collective-permute-done | bytes 917536 | tf_op jit(solution)/shard_map/ppermute | solution.py:128
  40.7 17.0 %collective-permute-done.3.refs_3_.refs_7_.refs_11_.refs_15_ = bf16[4,128,896]{2,1,0:T(8,128)(2,1)S(1)} collective-permute-done((bf16[4,128,896]{2,1,0:T(8,128)(2,1)}, bf16[4,128,896]{2,1,0:T(8,128)(2,1)S(1)}, u32[]{:S(2)}, u32[]{:S(2)}) %collective-permute-start.3) | collective-permute-done | bytes 917536 | tf_op jit(solution)/shard_map/ppermute | solution.py:128
  57.7 2.3 collective-permute-done
  60.1 4.7 %assemble.10 = (bf16[4,128,896]{2,1,0:T(8,128)(2,1)}, bf16[4,128,896]{2,1,0:T(8,128)(2,1)}, bf16[4,128,896]{2,1,0:T(8,128)(2,1)}, bf16[4,128,896]{2,1,0:T(8,128)(2,1)}, bf16[8,128,1024]{2,1,0:T(8,128)(2,1)}) custom-call(s32[1]{0:T(128)} %bitcast.m, bf16[128,53248]{1,0:T(8,128)(2,1)} %refs_12_.7, ...), custom_call_target="tpu_custom_call" | custom-call | flops 1 | bytes 1 | tf_op jit(solution)/shard_map/assemble/pallas_call | solution.py:63
  72.1 2.7 assemble.12
  74.7 68.5 %collective-permute-done.6.refs_2_.refs_3_.refs_6_.refs_7_.refs_10_.refs_11_.refs_14_.refs_15_ = bf16[8,128,1024]{2,1,0:T(8,128)(2,1)S(1)} collective-permute-done((bf16[8,128,1024]{2,1,0:T(8,128)(2,1)}, bf16[8,128,1024]{2,1,0:T(8,128)(2,1)S(1)}, u32[]{:S(2)}, u32[]{:S(2)}) %collective-permute-start.6) | collective-permute-done | bytes 2097184 | tf_op jit(solution)/shard_map/ppermute | solution.py:128
  144.6 3.8 assemble.11
  148.4 2.5 collective-permute-done.7.refs_8_.refs_9_.refs_10_.refs_11_
  152.5 2.8 collective-permute-start.12
  156.8 2.0 assemble.14
  158.8 66.5 %collective-permute-done.10.refs_2_.refs_3_.refs_6_.refs_7_.refs_10_.refs_11_.refs_14_.refs_15_ = bf16[8,128,1024]{2,1,0:T(8,128)(2,1)S(1)} collective-permute-done((bf16[8,128,1024]{2,1,0:T(8,128)(2,1)}, bf16[8,128,1024]{2,1,0:T(8,128)(2,1)S(1)}, u32[]{:S(2)}, u32[]{:S(2)}) %collective-permute-start.10) | collective-permute-done | bytes 2097184 | tf_op jit(solution)/shard_map/ppermute | solution.py:128
  226.7 3.8 assemble.13
  230.5 14.1 %collective-permute-start.15 = (bf16[4,128,1024]{2,1,0:T(8,128)(2,1)}, bf16[4,128,1024]{2,1,0:T(8,128)(2,1)S(1)}, u32[]{:S(2)}, u32[]{:S(2)}) collective-permute-start(bf16[4,128,1024]{2,1,0:T(8,128)(2,1)} %get-tuple-element.161), channel_id=1, source_target_pairs={{0,4},{1,5},{2,6},{3,7},{4,0},{5,1},{6,2},{7,3},{8,12},{9,13},{10,... | collective-permute-start | bytes 3145736 | tf_op jit(solution)/shard_map/ppermute | solution.py:128
  248.4 27.6 %collective-permute-done.14.refs_2_.refs_3_.refs_6_.refs_7_.refs_10_.refs_11_.refs_14_.refs_15_ = bf16[8,128,384]{2,1,0:T(8,128)(2,1)S(1)} collective-permute-done((bf16[8,128,384]{2,1,0:T(8,128)(2,1)S(1)}, bf16[8,128,384]{2,1,0:T(8,128)(2,1)S(1)}, u32[]{:S(2)}, u32[]{:S(2)}) %collective-permute-start.14) | collective-permute-done | bytes 786464 | tf_op jit(solution)/shard_map/ppermute | solution.py:128
  276.9 2.5 assemble.15
  279.5 24.0 %merge.4.refs_21_ = bf16[4096,3328]{1,0:T(8,128)(2,1)} custom-call(s32[1]{0:T(128)} %bitcast.m, bf16[512,4096]{1,0:T(8,128)(2,1)} %all-gather.5.cloned.1.call-done.refs_0_, bf16[512,4096]{1,0:T(8,128)(2,1)} %all-gather.7.cloned.1.call-done.refs_1_, bf16[512,4096]{1,0:T(8,128)(2,1)} %all-gather.9.cloned.1.call-done.refs_2_, ...), custom_call_target="tpu_custom_call" | custom-call | flops 1 | bytes 1 | tf_op jit(solution)/shard_map/merge/pallas_call | solution.py:108
  303.6 24.3 %merge.5.refs_21_ = bf16[4096,3328]{1,0:T(8,128)(2,1)} custom-call(s32[1]{0:T(128)} %bitcast.m, bf16[512,4096]{1,0:T(8,128)(2,1)} %all-gather.5.cloned.1.call-done.refs_0_, bf16[512,4096]{1,0:T(8,128)(2,1)} %all-gather.7.cloned.1.call-done.refs_1_, bf16[512,4096]{1,0:T(8,128)(2,1)} %all-gather.9.cloned.1.call-done.refs_2_, ...), custom_call_target="tpu_custom_call", output_to_operand_aliasing={{}: (22, {})} | custom-call | flops 1 | bytes 1 | tf_op jit(solution)/shard_map/merge/pallas_call | solution.py:108
  328.0 7.8 %collective-permute-start.18 = (bf16[4,128,384]{2,1,0:T(8,128)(2,1)S(1)}, bf16[4,128,384]{2,1,0:T(8,128)(2,1)S(1)}, u32[]{:S(2)}, u32[]{:S(2)}) collective-permute-start(bf16[4,128,384]{2,1,0:T(8,128)(2,1)S(1)} %copy-done.17), channel_id=1, source_target_pairs={{0,4},{1,5},{2,6},{3,7},{4,0},{5,1},{6,2},{7,3},{8,12},{9,13},{10,... | collective-permute-start | bytes 1179656 | tf_op jit(solution)/shard_map/ppermute | solution.py:128
  338.3 24.4 %merge.6.refs_21_ = bf16[4096,3328]{1,0:T(8,128)(2,1)} custom-call(s32[1]{0:T(128)} %bitcast.m, bf16[512,4096]{1,0:T(8,128)(2,1)} %all-gather.5.cloned.1.call-done.refs_0_, bf16[512,4096]{1,0:T(8,128)(2,1)} %all-gather.7.cloned.1.call-done.refs_1_, bf16[512,4096]{1,0:T(8,128)(2,1)} %all-gather.9.cloned.1.call-done.refs_2_, ...), custom_call_target="tpu_custom_call", output_to_operand_aliasing={{}: (22, {})} | custom-call | flops 1 | bytes 1 | tf_op jit(solution)/shard_map/merge/pallas_call | solution.py:108
  366.2 14.0 %merge.7 = bf16[4096,3328]{1,0:T(8,128)(2,1)} custom-call(s32[1]{0:T(128)} %bitcast.m, bf16[512,4096]{1,0:T(8,128)(2,1)} %all-gather.5.cloned.1.call-done.refs_0_, bf16[512,4096]{1,0:T(8,128)(2,1)} %all-gather.7.cloned.1.call-done.refs_1_, bf16[512,4096]{1,0:T(8,128)(2,1)} %all-gather.9.cloned.1.call-done.refs_2_, ...), custom_call_target="tpu_custom_call", output_to_operand_aliasing={{}: (22, {})} | custom-call | flops 1 | bytes 1 | tf_op jit(solution)/shard_map/merge/pallas_call | solution.py:108
  (81 shorter events, 28.2 us)
Async XLA Ops:
  6.5 272.9 %all-gather.9.cloned.1.call-start = ((), (), s32[]{:S(2)}) async-start(), calls=%async_computation.2 | async-start | bytes 5242880 | tf_op jit(solution)/shard_map/all_gather | solution.py:147
  8.8 48.9 %collective-permute-start.1 = (bf16[128,4096]{1,0:T(8,128)(2,1)S(1)}, bf16[128,4096]{1,0:T(8,128)(2,1)}, u32[]{:S(2)}, u32[]{:S(2)}) collective-permute-start(bf16[128,4096]{1,0:T(8,128)(2,1)S(1)} %multiply_convert_fusion), channel_id=1, source_target_pairs={{0,4},{1,5},{2,6},{3,7},{4,0},{5,1},{6,2},{7,3},{8,12},{9,13},{10,... | collective-permute-start | bytes 3145736 | tf_op jit(solution)/shard_map/ppermute | solution.py:128
  11.9 48.1 %collective-permute-start = (bf16[128,4096]{1,0:T(8,128)(2,1)S(1)}, bf16[128,4096]{1,0:T(8,128)(2,1)}, u32[]{:S(2)}, u32[]{:S(2)}) collective-permute-start(bf16[128,4096]{1,0:T(8,128)(2,1)S(1)} %multiply_convert_fusion), channel_id=1, source_target_pairs={{0,8},{1,9},{2,10},{3,11},{4,12},{5,13},{6,14},{7,15},{8,0},{9,1},... | collective-permute-start | bytes 3145736 | tf_op jit(solution)/shard_map/ppermute | solution.py:128
  18.7 39.0 %collective-permute-start.3 = (bf16[4,128,896]{2,1,0:T(8,128)(2,1)}, bf16[4,128,896]{2,1,0:T(8,128)(2,1)S(1)}, u32[]{:S(2)}, u32[]{:S(2)}) collective-permute-start(bf16[4,128,896]{2,1,0:T(8,128)(2,1)} %get-tuple-element.90), channel_id=1, source_target_pairs={{0,3},{1,2},{2,1},{3,0},{4,7},{5,6},{6,5},{7,4},{8,11},{9,10},{10,... | collective-permute-start | bytes 2752520 | tf_op jit(solution)/shard_map/ppermute | solution.py:128
  23.7 36.4 %collective-permute-start.4 = (bf16[8,128,3328]{2,1,0:T(8,128)(2,1)}, bf16[8,128,3328]{2,1,0:T(8,128)(2,1)}, u32[]{:S(2)}, u32[]{:S(2)}) collective-permute-start(bf16[8,128,3328]{2,1,0:T(8,128)(2,1)} %assemble.9), channel_id=1, source_target_pairs={{0,1},{1,0},{2,3},{3,2},{4,5},{5,4},{6,7},{7,6},{8,9},{9,8},{10,11... | collective-permute-start | bytes 20447240 | tf_op jit(solution)/shard_map/ppermute | solution.py:128
  60.0 219.4 %all-gather.5.cloned.1.call-start = ((), (), s32[]{:S(2)}) async-start(), calls=%async_computation | async-start | bytes 5242880 | tf_op jit(solution)/shard_map/all_gather | solution.py:147
  64.9 214.6 %all-gather.7.cloned.1.call-start = ((), (), s32[]{:S(2)}) async-start(), calls=%async_computation.1 | async-start | bytes 5242880 | tf_op jit(solution)/shard_map/all_gather | solution.py:147
  65.6 213.9 %all-gather.11.cloned.1.call-start = ((), (), s32[]{:S(2)}) async-start(), calls=%async_computation.3 | async-start | bytes 5242880 | tf_op jit(solution)/shard_map/all_gather | solution.py:147
  65.7 77.6 %collective-permute-start.6 = (bf16[8,128,1024]{2,1,0:T(8,128)(2,1)}, bf16[8,128,1024]{2,1,0:T(8,128)(2,1)S(1)}, u32[]{:S(2)}, u32[]{:S(2)}) collective-permute-start(bf16[8,128,1024]{2,1,0:T(8,128)(2,1)} %get-tuple-element.104), channel_id=1, source_target_pairs={{0,2},{1,3},{2,0},{3,1},{4,6},{5,7},{6,4},{7,5},{8,10},{9,11},{10,... | collective-permute-start | bytes 6291464 | tf_op jit(solution)/shard_map/ppermute | solution.py:128
  67.2 83.6 %collective-permute-start.5 = (bf16[128,4096]{1,0:T(8,128)(2,1)}, bf16[128,4096]{1,0:T(8,128)(2,1)S(1)}, u32[]{:S(2)}, u32[]{:S(2)}) collective-permute-start(bf16[128,4096]{1,0:T(8,128)(2,1)} %collective-permute-done), channel_id=1, source_target_pairs={{0,4},{1,5},{2,6},{3,7},{4,0},{5,1},{6,2},{7,3},{8,12},{9,13},{10,... | collective-permute-start | bytes 3145736 | tf_op jit(solution)/shard_map/ppermute | solution.py:128
  67.7 83.2 %collective-permute-start.7 = (bf16[4,128,896]{2,1,0:T(8,128)(2,1)}, bf16[4,128,896]{2,1,0:T(8,128)(2,1)}, u32[]{:S(2)}, u32[]{:S(2)}) collective-permute-start(bf16[4,128,896]{2,1,0:T(8,128)(2,1)} %get-tuple-element.110), channel_id=1, source_target_pairs={{0,4},{1,5},{2,6},{3,7},{4,0},{5,1},{6,2},{7,3},{8,12},{9,13},{10,... | collective-permute-start | bytes 2752520 | tf_op jit(solution)/shard_map/ppermute | solution.py:128
  69.2 81.6 %collective-permute-start.8 = (bf16[4,128,896]{2,1,0:T(8,128)(2,1)}, bf16[4,128,896]{2,1,0:T(8,128)(2,1)}, u32[]{:S(2)}, u32[]{:S(2)}) collective-permute-start(bf16[4,128,896]{2,1,0:T(8,128)(2,1)} %get-tuple-element.111), channel_id=1, source_target_pairs={{0,8},{1,9},{2,10},{3,11},{4,12},{5,13},{6,14},{7,15},{8,0},{9,1},... | collective-permute-start | bytes 2752520 | tf_op jit(solution)/shard_map/ppermute | solution.py:128
  70.3 80.6 %collective-permute-start.9 = (bf16[4,128,896]{2,1,0:T(8,128)(2,1)}, bf16[4,128,896]{2,1,0:T(8,128)(2,1)}, u32[]{:S(2)}, u32[]{:S(2)}) collective-permute-start(bf16[4,128,896]{2,1,0:T(8,128)(2,1)} %get-tuple-element.112), channel_id=1, source_target_pairs={{0,12},{1,13},{2,14},{3,15},{4,8},{5,9},{6,10},{7,11},{8,4},{9,5},... | collective-permute-start | bytes 2752520 | tf_op jit(solution)/shard_map/ppermute | solution.py:128
  151.8 73.5 %collective-permute-start.10 = (bf16[8,128,1024]{2,1,0:T(8,128)(2,1)}, bf16[8,128,1024]{2,1,0:T(8,128)(2,1)S(1)}, u32[]{:S(2)}, u32[]{:S(2)}) collective-permute-start(bf16[8,128,1024]{2,1,0:T(8,128)(2,1)} %assemble.12), channel_id=1, source_target_pairs={{0,2},{1,3},{2,0},{3,1},{4,6},{5,7},{6,4},{7,5},{8,10},{9,11},{10,... | collective-permute-start | bytes 6291464 | tf_op jit(solution)/shard_map/ppermute | solution.py:128
  152.5 78.0 %collective-permute-start.11 = (bf16[4,128,1024]{2,1,0:T(8,128)(2,1)}, bf16[4,128,1024]{2,1,0:T(8,128)(2,1)S(1)}, u32[]{:S(2)}, u32[]{:S(2)}) collective-permute-start(bf16[4,128,1024]{2,1,0:T(8,128)(2,1)} %get-tuple-element.132), channel_id=1, source_target_pairs={{0,4},{1,5},{2,6},{3,7},{4,0},{5,1},{6,2},{7,3},{8,12},{9,13},{10,... | collective-permute-start | bytes 3145736 | tf_op jit(solution)/shard_map/ppermute | solution.py:128
  152.5 78.0 %collective-permute-start.12 = (bf16[4,128,1024]{2,1,0:T(8,128)(2,1)}, bf16[4,128,1024]{2,1,0:T(8,128)(2,1)S(1)}, u32[]{:S(2)}, u32[]{:S(2)}) collective-permute-start(bf16[4,128,1024]{2,1,0:T(8,128)(2,1)} %get-tuple-element.133), channel_id=1, source_target_pairs={{0,8},{1,9},{2,10},{3,11},{4,12},{5,13},{6,14},{7,15},{8,0},{9,1},... | collective-permute-start | bytes 3145736 | tf_op jit(solution)/shard_map/ppermute | solution.py:128
  155.3 75.3 %collective-permute-start.13 = (bf16[4,128,1024]{2,1,0:T(8,128)(2,1)}, bf16[4,128,1024]{2,1,0:T(8,128)(2,1)S(1)}, u32[]{:S(2)}, u32[]{:S(2)}) collective-permute-start(bf16[4,128,1024]{2,1,0:T(8,128)(2,1)} %get-tuple-element.134), channel_id=1, source_target_pairs={{0,12},{1,13},{2,14},{3,15},{4,8},{5,9},{6,10},{7,11},{8,4},{9,5},... | collective-permute-start | bytes 3145736 | tf_op jit(solution)/shard_map/ppermute | solution.py:128
  230.5 97.4 %collective-permute-start.15 = (bf16[4,128,1024]{2,1,0:T(8,128)(2,1)}, bf16[4,128,1024]{2,1,0:T(8,128)(2,1)S(1)}, u32[]{:S(2)}, u32[]{:S(2)}) collective-permute-start(bf16[4,128,1024]{2,1,0:T(8,128)(2,1)} %get-tuple-element.161), channel_id=1, source_target_pairs={{0,4},{1,5},{2,6},{3,7},{4,0},{5,1},{6,2},{7,3},{8,12},{9,13},{10,... | collective-permute-start | bytes 3145736 | tf_op jit(solution)/shard_map/ppermute | solution.py:128
  244.6 83.4 %collective-permute-start.16 = (bf16[4,128,1024]{2,1,0:T(8,128)(2,1)}, bf16[4,128,1024]{2,1,0:T(8,128)(2,1)}, u32[]{:S(2)}, u32[]{:S(2)}) collective-permute-start(bf16[4,128,1024]{2,1,0:T(8,128)(2,1)} %get-tuple-element.162), channel_id=1, source_target_pairs={{0,8},{1,9},{2,10},{3,11},{4,12},{5,13},{6,14},{7,15},{8,0},{9,1},... | collective-permute-start | bytes 3145736 | tf_op jit(solution)/shard_map/ppermute | solution.py:128
  245.5 82.5 %collective-permute-start.17 = (bf16[4,128,1024]{2,1,0:T(8,128)(2,1)}, bf16[4,128,1024]{2,1,0:T(8,128)(2,1)}, u32[]{:S(2)}, u32[]{:S(2)}) collective-permute-start(bf16[4,128,1024]{2,1,0:T(8,128)(2,1)} %get-tuple-element.163), channel_id=1, source_target_pairs={{0,12},{1,13},{2,14},{3,15},{4,8},{5,9},{6,10},{7,11},{8,4},{9,5},... | collective-permute-start | bytes 3145736 | tf_op jit(solution)/shard_map/ppermute | solution.py:128
  247.0 29.1 %collective-permute-start.14 = (bf16[8,128,384]{2,1,0:T(8,128)(2,1)S(1)}, bf16[8,128,384]{2,1,0:T(8,128)(2,1)S(1)}, u32[]{:S(2)}, u32[]{:S(2)}) collective-permute-start(bf16[8,128,384]{2,1,0:T(8,128)(2,1)S(1)} %copy-done.14), channel_id=1, source_target_pairs={{0,2},{1,3},{2,0},{3,1},{4,6},{5,7},{6,4},{7,5},{8,10},{9,11},{10,... | collective-permute-start | bytes 2359304 | tf_op jit(solution)/shard_map/ppermute | solution.py:128
  328.0 34.8 %collective-permute-start.18 = (bf16[4,128,384]{2,1,0:T(8,128)(2,1)S(1)}, bf16[4,128,384]{2,1,0:T(8,128)(2,1)S(1)}, u32[]{:S(2)}, u32[]{:S(2)}) collective-permute-start(bf16[4,128,384]{2,1,0:T(8,128)(2,1)S(1)} %copy-done.17), channel_id=1, source_target_pairs={{0,4},{1,5},{2,6},{3,7},{4,0},{5,1},{6,2},{7,3},{8,12},{9,13},{10,... | collective-permute-start | bytes 1179656 | tf_op jit(solution)/shard_map/ppermute | solution.py:128
  335.8 28.8 %collective-permute-start.19 = (bf16[4,128,384]{2,1,0:T(8,128)(2,1)S(1)}, bf16[4,128,384]{2,1,0:T(8,128)(2,1)S(1)}, u32[]{:S(2)}, u32[]{:S(2)}) collective-permute-start(bf16[4,128,384]{2,1,0:T(8,128)(2,1)S(1)} %copy-done.16), channel_id=1, source_target_pairs={{0,8},{1,9},{2,10},{3,11},{4,12},{5,13},{6,14},{7,15},{8,0},{9,1},... | collective-permute-start | bytes 1179656 | tf_op jit(solution)/shard_map/ppermute | solution.py:128
  336.9 27.8 %collective-permute-start.20 = (bf16[4,128,384]{2,1,0:T(8,128)(2,1)S(1)}, bf16[4,128,384]{2,1,0:T(8,128)(2,1)S(1)}, u32[]{:S(2)}, u32[]{:S(2)}) collective-permute-start(bf16[4,128,384]{2,1,0:T(8,128)(2,1)S(1)} %copy-done.15), channel_id=1, source_target_pairs={{0,12},{1,13},{2,14},{3,15},{4,8},{5,9},{6,10},{7,11},{8,4},{9,5},... | collective-permute-start | bytes 1179656 | tf_op jit(solution)/shard_map/ppermute | solution.py:128
  (19 other events, 393.5 us)
Sparse Core Ops, SparseCore 0:
  60.2 57.1 all-gather.8
  118.9 45.2 all-gather.4
  165.7 59.9 all-gather.6
  227.2 45.3 all-gather.10

commit v5 on v4

--- a/solution.py
+++ b/solution.py
@@ -9,7 +9,7 @@
 RANK = 64
 UNIT = 128
 TILE = 1024
-SHARES = (7, 8, 8, 3)
+SHARES = (7, 8, 6, 3, 2)
 VMEM = 56 * 1024 * 1024
 NO_COST = pl.CostEstimate(flops=1, bytes_accessed=1, transcendentals=0)
 ANY = pl.BlockSpec(memory_space=pl.ANY)

time: 388 us -> 398 us (1.026)
  starting transfers between devices: 47.6 us -> 67.2 us
  waiting for transfers between devices: 203 us -> 184 us
  Pallas kernels: 114 us -> 123 us
    ppermute x21 -> x25, waiting for transfers between devices: 203 us -> 180 us  [swap(): return lax.ppermute(v, 'col', [(i, i ^ bit) for i in range(n)])]
    ppermute x21 -> x25, starting transfers between devices: 47.5 us -> 67.1 us  [swap(): return lax.ppermute(v, 'col', [(i, i ^ bit) for i in range(n)])]
    pallas_call x4 -> x5, Pallas kernels: 86.8 us -> 92.8 us  [merge(): pl.pallas_call(kernel, grid_spec=pltpu.PrefetchScalarGridSpec(num_scalar_...]
    pallas_call x8 -> x10, Pallas kernels: 27.1 us -> 30.5 us  [assemble(): pl.pallas_call(kernel, grid_spec=pltpu.PrefetchScalarGridSpec(num_scalar_...]
  transfers between devices with their start and end apart: 25 -> 29, of which waited for: 8 -> 12; matrix products, arithmetic and copies ran while one was open for 0% -> 0% of each run, Pallas kernels for 26% -> 28%
where the time goes in v5:
time: 398 us; the launch traced here: 397 us
  waiting for transfers between devices  184 us (46%)
  Pallas kernels  123 us (31%)
  starting transfers between devices  67.2 us (17%)
  between operations  13.4 us (3%)
  local copies, waits for them, and re-layouts  6.62 us (2%)
    ppermute x25, waiting for transfers between devices, swap(): return lax.ppermute(v, 'col', [(i, i ^ bit) for i in range(n)])  180 us
    pallas_call x5, Pallas kernels, merge(): pl.pallas_call(kernel, grid_spec=pltpu.PrefetchScalarGridSpec(num_scalar_...  92.8 us
    ppermute x25, starting transfers between devices, swap(): return lax.ppermute(v, 'col', [(i, i ^ bit) for i in range(n)])  67.1 us
    pallas_call x10, Pallas kernels, assemble(): pl.pallas_call(kernel, grid_spec=pltpu.PrefetchScalarGridSpec(num_scalar_...  30.5 us
  transfers between devices with their start and end apart: 29, of which 12 were waited for; matrix products, arithmetic and copies ran while one was open for 0% of the time, Pallas kernels for 28%

profile of v5, /device:TPU:0, one launch (start us, length us, event | category | flops | bytes accessed | tf_op | source)
XLA Modules:
  0.0 397.2 jit_solution(10297511579165735550)
XLA Ops:
  8.8 4.1 %collective-permute-start = (bf16[128,4096]{1,0:T(8,128)(2,1)S(1)}, bf16[128,4096]{1,0:T(8,128)(2,1)}, u32[]{:S(2)}, u32[]{:S(2)}) collective-permute-start(bf16[128,4096]{1,0:T(8,128)(2,1)S(1)} %multiply_convert_fusion), channel_id=1, source_target_pairs={{0,8},{1,9},{2,10},{3,11},{4,12},{5,13},{6,14},{7,15},{8,0},{9,1},... | collective-permute-start | bytes 3145736 | tf_op jit(solution)/shard_map/ppermute | solution.py:128
  14.5 2.6 assemble.10
  18.7 5.1 %assemble.11 = bf16[8,128,3328]{2,1,0:T(8,128)(2,1)} custom-call(s32[1]{0:T(128)} %bitcast.m, bf16[128,53248]{1,0:T(8,128)(2,1)} %refs_12_.9, bf16[128,53248]{1,0:T(8,128)(2,1)} %refs_12_.9, bf16[128,53248]{1,0:T(8,128)(2,1)} %refs_12_.9, bf16[128,53248]{1,0:T(8,128)(2,1)} %refs_12_.9, bf16[128,53248]{1,0:T(8,128)(2,1)} %refs_12_.9, ...), custom_call_target="tpu_custom_call" | custom-call | flops 1 | bytes 1 | tf_op jit(solution)/shard_map/assemble/pallas_call | solution.py:63
  24.3 16.3 %collective-permute-done.2.refs_2_.refs_6_.refs_10_.refs_14_ = bf16[4,128,896]{2,1,0:T(8,128)(2,1)S(1)} collective-permute-done((bf16[4,128,896]{2,1,0:T(8,128)(2,1)}, bf16[4,128,896]{2,1,0:T(8,128)(2,1)S(1)}, u32[]{:S(2)}, u32[]{:S(2)}) %collective-permute-start.2) | collective-permute-done | bytes 917536 | tf_op jit(solution)/shard_map/ppermute | solution.py:128
  40.7 17.0 %collective-permute-done.3.refs_3_.refs_7_.refs_11_.refs_15_ = bf16[4,128,896]{2,1,0:T(8,128)(2,1)S(1)} collective-permute-done((bf16[4,128,896]{2,1,0:T(8,128)(2,1)}, bf16[4,128,896]{2,1,0:T(8,128)(2,1)S(1)}, u32[]{:S(2)}, u32[]{:S(2)}) %collective-permute-start.3) | collective-permute-done | bytes 917536 | tf_op jit(solution)/shard_map/ppermute | solution.py:128
  59.0 4.7 %assemble.12 = (bf16[4,128,896]{2,1,0:T(8,128)(2,1)}, bf16[4,128,896]{2,1,0:T(8,128)(2,1)}, bf16[4,128,896]{2,1,0:T(8,128)(2,1)}, bf16[4,128,896]{2,1,0:T(8,128)(2,1)}, bf16[8,128,1024]{2,1,0:T(8,128)(2,1)}) custom-call(s32[1]{0:T(128)} %bitcast.m, bf16[128,53248]{1,0:T(8,128)(2,1)} %refs_12_.9, ...), custom_call_target="tpu_custom_call" | custom-call | flops 1 | bytes 1 | tf_op jit(solution)/shard_map/assemble/pallas_call | solution.py:63
  74.4 68.1 %collective-permute-done.6.refs_2_.refs_3_.refs_6_.refs_7_.refs_10_.refs_11_.refs_14_.refs_15_ = bf16[8,128,1024]{2,1,0:T(8,128)(2,1)S(1)} collective-permute-done((bf16[8,128,1024]{2,1,0:T(8,128)(2,1)}, bf16[8,128,1024]{2,1,0:T(8,128)(2,1)S(1)}, u32[]{:S(2)}, u32[]{:S(2)}) %collective-permute-start.6) | collective-permute-done | bytes 2097184 | tf_op jit(solution)/shard_map/ppermute | solution.py:128
  143.8 3.9 assemble.13
  147.8 4.0 collective-permute-done.9.refs_16_.refs_17_.refs_18_.refs_19_
  159.7 46.5 %collective-permute-done.10.refs_2_.refs_3_.refs_6_.refs_7_.refs_10_.refs_11_.refs_14_.refs_15_ = bf16[8,128,768]{2,1,0:T(8,128)(2,1)S(1)} collective-permute-done((bf16[8,128,768]{2,1,0:T(8,128)(2,1)S(1)}, bf16[8,128,768]{2,1,0:T(8,128)(2,1)S(1)}, u32[]{:S(2)}, u32[]{:S(2)}) %collective-permute-start.10) | collective-permute-done | bytes 1572896 | tf_op jit(solution)/shard_map/ppermute | solution.py:128
  207.3 3.3 assemble.15
  210.6 14.8 %collective-permute-done.12.refs_12_.refs_13_.refs_14_.refs_15_ = bf16[4,128,1024]{2,1,0:T(8,128)(2,1)S(1)} collective-permute-done((bf16[4,128,1024]{2,1,0:T(8,128)(2,1)}, bf16[4,128,1024]{2,1,0:T(8,128)(2,1)S(1)}, u32[]{:S(2)}, u32[]{:S(2)}) %collective-permute-start.12) | collective-permute-done | bytes 1048608 | tf_op jit(solution)/shard_map/ppermute | solution.py:128
  227.1 20.9 %collective-permute-start.15 = (bf16[4,128,768]{2,1,0:T(8,128)(2,1)}, bf16[4,128,768]{2,1,0:T(8,128)(2,1)}, u32[]{:S(2)}, u32[]{:S(2)}) collective-permute-start(bf16[4,128,768]{2,1,0:T(8,128)(2,1)} %get-tuple-element.175), channel_id=1, source_target_pairs={{0,4},{1,5},{2,6},{3,7},{4,0},{5,1},{6,2},{7,3},{8,12},{9,13},{10,... | collective-permute-start | bytes 2359304 | tf_op jit(solution)/shard_map/ppermute | solution.py:128
  252.1 3.5 collective-permute-done.14.refs_2_.refs_3_.refs_6_.refs_7_.refs_10_.refs_11_.refs_14_.refs_15_
  259.1 3.2 all-gather.11.cloned.1.call-done.refs_3_
  262.3 24.1 %merge.5.refs_21_ = bf16[4096,3328]{1,0:T(8,128)(2,1)} custom-call(s32[1]{0:T(128)} %bitcast.m, bf16[512,4096]{1,0:T(8,128)(2,1)} %all-gather.5.cloned.1.call-done.refs_0_, bf16[512,4096]{1,0:T(8,128)(2,1)} %all-gather.7.cloned.1.call-done.refs_1_, bf16[512,4096]{1,0:T(8,128)(2,1)} %all-gather.9.cloned.1.call-done.refs_2_, ...), custom_call_target="tpu_custom_call" | custom-call | flops 1 | bytes 1 | tf_op jit(solution)/shard_map/merge/pallas_call | solution.py:108
  286.4 24.3 %merge.6.refs_21_ = bf16[4096,3328]{1,0:T(8,128)(2,1)} custom-call(s32[1]{0:T(128)} %bitcast.m, bf16[512,4096]{1,0:T(8,128)(2,1)} %all-gather.5.cloned.1.call-done.refs_0_, bf16[512,4096]{1,0:T(8,128)(2,1)} %all-gather.7.cloned.1.call-done.refs_1_, bf16[512,4096]{1,0:T(8,128)(2,1)} %all-gather.9.cloned.1.call-done.refs_2_, ...), custom_call_target="tpu_custom_call", output_to_operand_aliasing={{}: (22, {})} | custom-call | flops 1 | bytes 1 | tf_op jit(solution)/shard_map/merge/pallas_call | solution.py:108
  312.4 9.0 %collective-permute-start.19 = (bf16[4,128,384]{2,1,0:T(8,128)(2,1)S(1)}, bf16[4,128,384]{2,1,0:T(8,128)(2,1)S(1)}, u32[]{:S(2)}, u32[]{:S(2)}) collective-permute-start(bf16[4,128,384]{2,1,0:T(8,128)(2,1)S(1)} %copy-done.22), channel_id=1, source_target_pairs={{0,4},{1,5},{2,6},{3,7},{4,0},{5,1},{6,2},{7,3},{8,12},{9,13},{10,... | collective-permute-start | bytes 1179656 | tf_op jit(solution)/shard_map/ppermute | solution.py:128
  323.8 19.8 %merge.7.refs_21_ = bf16[4096,3328]{1,0:T(8,128)(2,1)} custom-call(s32[1]{0:T(128)} %bitcast.m, bf16[512,4096]{1,0:T(8,128)(2,1)} %all-gather.5.cloned.1.call-done.refs_0_, bf16[512,4096]{1,0:T(8,128)(2,1)} %all-gather.7.cloned.1.call-done.refs_1_, bf16[512,4096]{1,0:T(8,128)(2,1)} %all-gather.9.cloned.1.call-done.refs_2_, ...), custom_call_target="tpu_custom_call", output_to_operand_aliasing={{}: (22, {})} | custom-call | flops 1 | bytes 1 | tf_op jit(solution)/shard_map/merge/pallas_call | solution.py:108
  346.7 4.5 %collective-permute-done.20.refs_12_.refs_13_.refs_14_.refs_15_ = bf16[4,128,384]{2,1,0:T(8,128)(2,1)S(1)} collective-permute-done((bf16[4,128,384]{2,1,0:T(8,128)(2,1)S(1)}, bf16[4,128,384]{2,1,0:T(8,128)(2,1)S(1)}, u32[]{:S(2)}, u32[]{:S(2)}) %collective-permute-start.20) | collective-permute-done | bytes 393248 | tf_op jit(solution)/shard_map/ppermute | solution.py:128
  351.2 6.7 %collective-permute-start.22 = (bf16[4,128,256]{2,1,0:T(8,128)(2,1)}, bf16[4,128,256]{2,1,0:T(8,128)(2,1)S(1)}, u32[]{:S(2)}, u32[]{:S(2)}) collective-permute-start(bf16[4,128,256]{2,1,0:T(8,128)(2,1)} %get-tuple-element.193), channel_id=1, source_target_pairs={{0,4},{1,5},{2,6},{3,7},{4,0},{5,1},{6,2},{7,3},{8,12},{9,13},{10,... | collective-permute-start | bytes 786440 | tf_op jit(solution)/shard_map/ppermute | solution.py:128
  360.3 14.1 %merge.8.refs_21_ = bf16[4096,3328]{1,0:T(8,128)(2,1)} custom-call(s32[1]{0:T(128)} %bitcast.m, bf16[512,4096]{1,0:T(8,128)(2,1)} %all-gather.5.cloned.1.call-done.refs_0_, bf16[512,4096]{1,0:T(8,128)(2,1)} %all-gather.7.cloned.1.call-done.refs_1_, bf16[512,4096]{1,0:T(8,128)(2,1)} %all-gather.9.cloned.1.call-done.refs_2_, ...), custom_call_target="tpu_custom_call", output_to_operand_aliasing={{}: (22, {})} | custom-call | flops 1 | bytes 1 | tf_op jit(solution)/shard_map/merge/pallas_call | solution.py:108
  374.4 4.4 %collective-permute-done.23.refs_12_.refs_13_.refs_14_.refs_15_ = bf16[4,128,256]{2,1,0:T(8,128)(2,1)S(1)} collective-permute-done((bf16[4,128,256]{2,1,0:T(8,128)(2,1)}, bf16[4,128,256]{2,1,0:T(8,128)(2,1)S(1)}, u32[]{:S(2)}, u32[]{:S(2)}) %collective-permute-start.23) | collective-permute-done | bytes 262176 | tf_op jit(solution)/shard_map/ppermute | solution.py:128
  380.1 10.5 %merge.9 = bf16[4096,3328]{1,0:T(8,128)(2,1)} custom-call(s32[1]{0:T(128)} %bitcast.m, bf16[512,4096]{1,0:T(8,128)(2,1)} %all-gather.5.cloned.1.call-done.refs_0_, bf16[512,4096]{1,0:T(8,128)(2,1)} %all-gather.7.cloned.1.call-done.refs_1_, bf16[512,4096]{1,0:T(8,128)(2,1)} %all-gather.9.cloned.1.call-done.refs_2_, ...), custom_call_target="tpu_custom_call", output_to_operand_aliasing={{}: (22, {})} | custom-call | flops 1 | bytes 1 | tf_op jit(solution)/shard_map/merge/pallas_call | solution.py:108
  (102 shorter events, 48.3 us)
Async XLA Ops:
  6.5 252.5 %all-gather.9.cloned.1.call-start = ((), (), s32[]{:S(2)}) async-start(), calls=%async_computation.2 | async-start | bytes 5242880 | tf_op jit(solution)/shard_map/all_gather | solution.py:147
  8.8 49.9 %collective-permute-start = (bf16[128,4096]{1,0:T(8,128)(2,1)S(1)}, bf16[128,4096]{1,0:T(8,128)(2,1)}, u32[]{:S(2)}, u32[]{:S(2)}) collective-permute-start(bf16[128,4096]{1,0:T(8,128)(2,1)S(1)} %multiply_convert_fusion), channel_id=1, source_target_pairs={{0,8},{1,9},{2,10},{3,11},{4,12},{5,13},{6,14},{7,15},{8,0},{9,1},... | collective-permute-start | bytes 3145736 | tf_op jit(solution)/shard_map/ppermute | solution.py:128
  12.9 46.0 %collective-permute-start.1 = (bf16[128,4096]{1,0:T(8,128)(2,1)S(1)}, bf16[128,4096]{1,0:T(8,128)(2,1)}, u32[]{:S(2)}, u32[]{:S(2)}) collective-permute-start(bf16[128,4096]{1,0:T(8,128)(2,1)S(1)} %multiply_convert_fusion), channel_id=1, source_target_pairs={{0,4},{1,5},{2,6},{3,7},{4,0},{5,1},{6,2},{7,3},{8,12},{9,13},{10,... | collective-permute-start | bytes 3145736 | tf_op jit(solution)/shard_map/ppermute | solution.py:128
  18.7 39.0 %collective-permute-start.3 = (bf16[4,128,896]{2,1,0:T(8,128)(2,1)}, bf16[4,128,896]{2,1,0:T(8,128)(2,1)S(1)}, u32[]{:S(2)}, u32[]{:S(2)}) collective-permute-start(bf16[4,128,896]{2,1,0:T(8,128)(2,1)} %get-tuple-element.104), channel_id=1, source_target_pairs={{0,3},{1,2},{2,1},{3,0},{4,7},{5,6},{6,5},{7,4},{8,11},{9,10},{10,... | collective-permute-start | bytes 2752520 | tf_op jit(solution)/shard_map/ppermute | solution.py:128
  23.7 35.3 %collective-permute-start.4 = (bf16[8,128,3328]{2,1,0:T(8,128)(2,1)}, bf16[8,128,3328]{2,1,0:T(8,128)(2,1)}, u32[]{:S(2)}, u32[]{:S(2)}) collective-permute-start(bf16[8,128,3328]{2,1,0:T(8,128)(2,1)} %assemble.11), channel_id=1, source_target_pairs={{0,1},{1,0},{2,3},{3,2},{4,5},{5,4},{6,7},{7,6},{8,9},{9,8},{10,11... | collective-permute-start | bytes 20447240 | tf_op jit(solution)/shard_map/ppermute | solution.py:128
  58.9 200.1 %all-gather.5.cloned.1.call-start = ((), (), s32[]{:S(2)}) async-start(), calls=%async_computation | async-start | bytes 5242880 | tf_op jit(solution)/shard_map/all_gather | solution.py:147
  63.8 195.3 %all-gather.7.cloned.1.call-start = ((), (), s32[]{:S(2)}) async-start(), calls=%async_computation.1 | async-start | bytes 5242880 | tf_op jit(solution)/shard_map/all_gather | solution.py:147
  64.5 197.7 %all-gather.11.cloned.1.call-start = ((), (), s32[]{:S(2)}) async-start(), calls=%async_computation.3 | async-start | bytes 5242880 | tf_op jit(solution)/shard_map/all_gather | solution.py:147
  64.6 77.9 %collective-permute-start.6 = (bf16[8,128,1024]{2,1,0:T(8,128)(2,1)}, bf16[8,128,1024]{2,1,0:T(8,128)(2,1)S(1)}, u32[]{:S(2)}, u32[]{:S(2)}) collective-permute-start(bf16[8,128,1024]{2,1,0:T(8,128)(2,1)} %get-tuple-element.118), channel_id=1, source_target_pairs={{0,2},{1,3},{2,0},{3,1},{4,6},{5,7},{6,4},{7,5},{8,10},{9,11},{10,... | collective-permute-start | bytes 6291464 | tf_op jit(solution)/shard_map/ppermute | solution.py:128
  66.2 85.6 %collective-permute-start.5 = (bf16[128,4096]{1,0:T(8,128)(2,1)}, bf16[128,4096]{1,0:T(8,128)(2,1)S(1)}, u32[]{:S(2)}, u32[]{:S(2)}) collective-permute-start(bf16[128,4096]{1,0:T(8,128)(2,1)} %collective-permute-done), channel_id=1, source_target_pairs={{0,4},{1,5},{2,6},{3,7},{4,0},{5,1},{6,2},{7,3},{8,12},{9,13},{10,... | collective-permute-start | bytes 3145736 | tf_op jit(solution)/shard_map/ppermute | solution.py:128
  67.6 80.1 %collective-permute-start.7 = (bf16[4,128,896]{2,1,0:T(8,128)(2,1)}, bf16[4,128,896]{2,1,0:T(8,128)(2,1)}, u32[]{:S(2)}, u32[]{:S(2)}) collective-permute-start(bf16[4,128,896]{2,1,0:T(8,128)(2,1)} %get-tuple-element.124), channel_id=1, source_target_pairs={{0,4},{1,5},{2,6},{3,7},{4,0},{5,1},{6,2},{7,3},{8,12},{9,13},{10,... | collective-permute-start | bytes 2752520 | tf_op jit(solution)/shard_map/ppermute | solution.py:128
  68.2 79.5 %collective-permute-start.8 = (bf16[4,128,896]{2,1,0:T(8,128)(2,1)}, bf16[4,128,896]{2,1,0:T(8,128)(2,1)}, u32[]{:S(2)}, u32[]{:S(2)}) collective-permute-start(bf16[4,128,896]{2,1,0:T(8,128)(2,1)} %get-tuple-element.125), channel_id=1, source_target_pairs={{0,8},{1,9},{2,10},{3,11},{4,12},{5,13},{6,14},{7,15},{8,0},{9,1},... | collective-permute-start | bytes 2752520 | tf_op jit(solution)/shard_map/ppermute | solution.py:128
  70.0 81.8 %collective-permute-start.9 = (bf16[4,128,896]{2,1,0:T(8,128)(2,1)}, bf16[4,128,896]{2,1,0:T(8,128)(2,1)}, u32[]{:S(2)}, u32[]{:S(2)}) collective-permute-start(bf16[4,128,896]{2,1,0:T(8,128)(2,1)} %get-tuple-element.126), channel_id=1, source_target_pairs={{0,12},{1,13},{2,14},{3,15},{4,8},{5,9},{6,10},{7,11},{8,4},{9,5},... | collective-permute-start | bytes 2752520 | tf_op jit(solution)/shard_map/ppermute | solution.py:128
  152.7 53.5 %collective-permute-start.10 = (bf16[8,128,768]{2,1,0:T(8,128)(2,1)S(1)}, bf16[8,128,768]{2,1,0:T(8,128)(2,1)S(1)}, u32[]{:S(2)}, u32[]{:S(2)}) collective-permute-start(bf16[8,128,768]{2,1,0:T(8,128)(2,1)S(1)} %copy-done.16), channel_id=1, source_target_pairs={{0,2},{1,3},{2,0},{3,1},{4,6},{5,7},{6,4},{7,5},{8,10},{9,11},{10,... | collective-permute-start | bytes 4718600 | tf_op jit(solution)/shard_map/ppermute | solution.py:128
  153.3 57.3 %collective-permute-start.11 = (bf16[4,128,1024]{2,1,0:T(8,128)(2,1)}, bf16[4,128,1024]{2,1,0:T(8,128)(2,1)S(1)}, u32[]{:S(2)}, u32[]{:S(2)}) collective-permute-start(bf16[4,128,1024]{2,1,0:T(8,128)(2,1)} %get-tuple-element.146), channel_id=1, source_target_pairs={{0,4},{1,5},{2,6},{3,7},{4,0},{5,1},{6,2},{7,3},{8,12},{9,13},{10,... | collective-permute-start | bytes 3145736 | tf_op jit(solution)/shard_map/ppermute | solution.py:128
  153.3 72.1 %collective-permute-start.12 = (bf16[4,128,1024]{2,1,0:T(8,128)(2,1)}, bf16[4,128,1024]{2,1,0:T(8,128)(2,1)S(1)}, u32[]{:S(2)}, u32[]{:S(2)}) collective-permute-start(bf16[4,128,1024]{2,1,0:T(8,128)(2,1)} %get-tuple-element.147), channel_id=1, source_target_pairs={{0,8},{1,9},{2,10},{3,11},{4,12},{5,13},{6,14},{7,15},{8,0},{9,1},... | collective-permute-start | bytes 3145736 | tf_op jit(solution)/shard_map/ppermute | solution.py:128
  155.7 69.8 %collective-permute-start.13 = (bf16[4,128,1024]{2,1,0:T(8,128)(2,1)}, bf16[4,128,1024]{2,1,0:T(8,128)(2,1)S(1)}, u32[]{:S(2)}, u32[]{:S(2)}) collective-permute-start(bf16[4,128,1024]{2,1,0:T(8,128)(2,1)} %get-tuple-element.148), channel_id=1, source_target_pairs={{0,12},{1,13},{2,14},{3,15},{4,8},{5,9},{6,10},{7,11},{8,4},{9,5},... | collective-permute-start | bytes 3145736 | tf_op jit(solution)/shard_map/ppermute | solution.py:128
  225.5 30.1 %collective-permute-start.14 = (bf16[8,128,384]{2,1,0:T(8,128)(2,1)S(1)}, bf16[8,128,384]{2,1,0:T(8,128)(2,1)S(1)}, u32[]{:S(2)}, u32[]{:S(2)}) collective-permute-start(bf16[8,128,384]{2,1,0:T(8,128)(2,1)S(1)} %copy-done.18), channel_id=1, source_target_pairs={{0,2},{1,3},{2,0},{3,1},{4,6},{5,7},{6,4},{7,5},{8,10},{9,11},{10,... | collective-permute-start | bytes 2359304 | tf_op jit(solution)/shard_map/ppermute | solution.py:128
  227.1 83.7 %collective-permute-start.15 = (bf16[4,128,768]{2,1,0:T(8,128)(2,1)}, bf16[4,128,768]{2,1,0:T(8,128)(2,1)}, u32[]{:S(2)}, u32[]{:S(2)}) collective-permute-start(bf16[4,128,768]{2,1,0:T(8,128)(2,1)} %get-tuple-element.175), channel_id=1, source_target_pairs={{0,4},{1,5},{2,6},{3,7},{4,0},{5,1},{6,2},{7,3},{8,12},{9,13},{10,... | collective-permute-start | bytes 2359304 | tf_op jit(solution)/shard_map/ppermute | solution.py:128
  247.9 62.9 %collective-permute-start.16 = (bf16[4,128,768]{2,1,0:T(8,128)(2,1)}, bf16[4,128,768]{2,1,0:T(8,128)(2,1)}, u32[]{:S(2)}, u32[]{:S(2)}) collective-permute-start(bf16[4,128,768]{2,1,0:T(8,128)(2,1)} %get-tuple-element.176), channel_id=1, source_target_pairs={{0,8},{1,9},{2,10},{3,11},{4,12},{5,13},{6,14},{7,15},{8,0},{9,1},... | collective-permute-start | bytes 2359304 | tf_op jit(solution)/shard_map/ppermute | solution.py:128
  247.9 62.9 %collective-permute-start.17 = (bf16[4,128,768]{2,1,0:T(8,128)(2,1)}, bf16[4,128,768]{2,1,0:T(8,128)(2,1)}, u32[]{:S(2)}, u32[]{:S(2)}) collective-permute-start(bf16[4,128,768]{2,1,0:T(8,128)(2,1)} %get-tuple-element.177), channel_id=1, source_target_pairs={{0,12},{1,13},{2,14},{3,15},{4,8},{5,9},{6,10},{7,11},{8,4},{9,5},... | collective-permute-start | bytes 2359304 | tf_op jit(solution)/shard_map/ppermute | solution.py:128
  310.8 32.8 %collective-permute-start.18 = (bf16[8,128,256]{2,1,0:T(8,128)(2,1)S(1)}, bf16[8,128,256]{2,1,0:T(8,128)(2,1)S(1)}, u32[]{:S(2)}, u32[]{:S(2)}) collective-permute-start(bf16[8,128,256]{2,1,0:T(8,128)(2,1)S(1)} %copy-done.19), channel_id=1, source_target_pairs={{0,2},{1,3},{2,0},{3,1},{4,6},{5,7},{6,4},{7,5},{8,10},{9,11},{10,... | collective-permute-start | bytes 1572872 | tf_op jit(solution)/shard_map/ppermute | solution.py:128
  312.4 34.3 %collective-permute-start.19 = (bf16[4,128,384]{2,1,0:T(8,128)(2,1)S(1)}, bf16[4,128,384]{2,1,0:T(8,128)(2,1)S(1)}, u32[]{:S(2)}, u32[]{:S(2)}) collective-permute-start(bf16[4,128,384]{2,1,0:T(8,128)(2,1)S(1)} %copy-done.22), channel_id=1, source_target_pairs={{0,4},{1,5},{2,6},{3,7},{4,0},{5,1},{6,2},{7,3},{8,12},{9,13},{10,... | collective-permute-start | bytes 1179656 | tf_op jit(solution)/shard_map/ppermute | solution.py:128
  321.4 29.8 %collective-permute-start.20 = (bf16[4,128,384]{2,1,0:T(8,128)(2,1)S(1)}, bf16[4,128,384]{2,1,0:T(8,128)(2,1)S(1)}, u32[]{:S(2)}, u32[]{:S(2)}) collective-permute-start(bf16[4,128,384]{2,1,0:T(8,128)(2,1)S(1)} %copy-done.21), channel_id=1, source_target_pairs={{0,8},{1,9},{2,10},{3,11},{4,12},{5,13},{6,14},{7,15},{8,0},{9,1},... | collective-permute-start | bytes 1179656 | tf_op jit(solution)/shard_map/ppermute | solution.py:128
  (28 other events, 547.0 us)
Sparse Core Ops, SparseCore 0:
  59.1 57.9 all-gather.8
  118.6 43.8 all-gather.4
  164.0 51.7 all-gather.6
  217.2 45.0 all-gather.10
